TPU v7x, 128 devices: a whole 4x4x4 slice. The times are simulated.
128 devices in a mesh: row: 32 (over x, z, core), col: 4 (over y).
Axes of the slice: x: 4, y: 4, z: 4, core: 2. Of those that a mesh axis runs over, the one named last changes fastest.
Arguments:
- influence: float32 [131072, 1024], P('row', 'col'), may hold values from -320 to 320, as said below
Outputs:
- factored: float32 [131072, 1024], P('row', 'col')
- upper: float32 [512, 1024], P(None, 'col')
Inputs may be any that keep to these rules, and one draw needn't show every extreme that they name: `influence`: real-valued samples.
All inputs are finite; a program needn't handle non-finite values.
Results may differ from a plain program's by a relative error of at most 0.000068.
Values sent between devices are 32-bit elements; how exact they have to be, the bound alone decides.
A program may use at most 128 MiB of HBM per device.

v0:
```python
import jax
import jax.numpy as jnp
from jax import lax
from jax.sharding import PartitionSpec as P


def partner_2(block, axis, distance):
    count = lax.axis_size(axis)
    route = []
    for low in range(count):
        high = low | 1 << distance
        if high != low and high < count:
            route += [(low, high), (high, low)]
    return lax.ppermute(block, axis, route)


def from_root(value, axis, source):
    kept = jnp.where(lax.axis_index(axis) == source, value, 0).astype(value.dtype)
    return lax.psum(kept, axis)


def factor_panel(block, total_rows):
    gram = (
        lax.dot_general(block, block, (((0,), (0,)), ((), ())), precision=lax.Precision.HIGHEST)
        / total_rows
    )
    levels = lax.axis_size("row").bit_length() - 1
    for level in range(levels):
        partner = partner_2(gram, "row", level)
        gram = gram + partner
    lower = jnp.linalg.cholesky(gram)
    eye = jnp.eye(block.shape[1], dtype=jnp.float32)
    inverse = lax.linalg.triangular_solve(lower, eye, left_side=True, lower=True)
    basis = lax.dot_general(
        block, inverse, (((1,), (1,)), ((), ())), precision=lax.Precision.HIGHEST
    )
    return (lower, basis)


def inner_products(basis, block, total_rows):
    return (
        lax.dot_general(basis, block, (((0,), (0,)), ((), ())), precision=lax.Precision.HIGHEST)
        / total_rows
    )


def on_device(influence):
    total_rows = influence.shape[0] * lax.axis_size("row")
    column = lax.axis_index("col")
    lower1, own_basis = factor_panel(influence, total_rows)
    basis1 = from_root(own_basis, "col", 0)
    coeff1 = lax.psum(inner_products(basis1, influence, total_rows), "row")
    rest1 = influence - jnp.dot(basis1, coeff1, precision=lax.Precision.HIGHEST)
    source = jnp.where(column == 0, influence, rest1)
    lower2, own_second = factor_panel(source, total_rows)
    basis2 = from_root(own_second, "col", 1)
    coeff2 = lax.psum(inner_products(basis2, rest1, total_rows), "row")
    tail2 = rest1 - jnp.dot(basis2, coeff2, precision=lax.Precision.HIGHEST)
    factored = jnp.where(column == 0, basis1, jnp.where(column == 1, basis2, tail2))
    top_rows = jnp.where(column == 0, lower1.T, coeff1)
    bottom_rows = jnp.where(
        column == 0, jnp.zeros_like(coeff2), jnp.where(column == 1, lower2.T, coeff2)
    )
    upper = jnp.concatenate([top_rows, bottom_rows], axis=0)
    return (factored, upper)


def solution(mesh):
    placed = (P("row", "col"),)
    return jax.shard_map(
        on_device,
        mesh=mesh,
        in_specs=placed,
        out_specs=(P("row", "col"), P(None, "col")),
        check_vma=False,
    )
```

profile of v0, /device:TPU:17, one launch (start us, length us, event | category | flops | bytes accessed | tf_op | source)
XLA Modules:
  0.0 678.0 jit_solution(5569080908325276058)
XLA Ops:
  7.2 10.2 %convolution_multiply_fusion.2 = f32[256,256]{0,1:T(8,128)S(1)} fusion(f32[4096,256]{1,0:T(8,128)} %param.4), kind=kOutput, calls=%fused_computation.16 | convolution fusion | flops 3221291008 | bytes 4456448 | tf_op jit(solution)/shard_map/dot_general | solution.py:24
  17.4 0.8 collective-permute-start
  18.2 1.2 collective-permute-done
  19.4 1.7 collective-permute-start.1
  21.1 6.3 collective-permute-done.1
  27.4 3.3 collective-permute-start.2
  30.7 5.4 collective-permute-done.2
  36.2 1.3 collective-permute-start.3
  37.5 4.8 collective-permute-done.3
  42.3 3.0 collective-permute-start.4
  45.3 4.0 collective-permute-done.4
  49.5 11.7 %cholesky.130 = f32[128,128]{1,0:T(8,128)S(1)} custom-call(f32[128,128]{1,0:T(8,128)S(1)} %cholesky.194), custom_call_target="Cholesky" | custom-call | tf_op jit(solution)/shard_map/jit(cholesky)/cholesky | solution.py:31
  61.3 9.8 %custom-call.13 = f32[1,128,128]{1,2,0:T(8,128)S(1)} custom-call(f32[1,128,128]{2,1,0:T(8,128)S(1)} %get-tuple-element.49), custom_call_target="InvertDiagBlocksLowerTriangular" | custom-call | tf_op jit(solution)/shard_map/jit(cholesky)/cholesky | solution.py:31
  71.8 11.7 %cholesky.147 = f32[128,128]{1,0:T(8,128)S(1)} custom-call(f32[128,128]{1,0:T(8,128)S(1)} %slice_subtract_fusion.1), custom_call_target="Cholesky" | custom-call | tf_op jit(solution)/shard_map/jit(cholesky)/cholesky | solution.py:31
  85.8 4.5 while.4
  86.8 1.4 bitcast_dynamic-update-slice_fusion.4
  88.8 1.4 bitcast_dynamic-update-slice_fusion.4
  90.3 19.7 %custom-call.14 = f32[2,128,128]{1,2,0:T(8,128)S(1)} custom-call(f32[2,128,128]{2,1,0:T(8,128)S(1)} %get-tuple-element.18), custom_call_target="InvertDiagBlocksLowerTriangular" | custom-call | tf_op jit(solution)/shard_map/triangular_solve/custom-call.0 | solution.py:33
  110.9 12.2 %fusion = f32[4096,256]{0,1:T(8,128)} fusion(f32[4096,256]{1,0:T(8,128)} %param.4, pred[]{:T(512)S(6)} %eq.8, f32[128,256]{1,0:T(8,128)S(1)} %fusion.27, f32[128,256]{1,0:T(8,128)S(1)} %fusion.20), kind=kOutput, calls=%fused_computation.6 | convolution fusion | flops 3222339584 | bytes 8650753 | tf_op jit(solution)/shard_map/dot_general | solution.py:34
  123.1 96.0 %all-reduce.6.cloned.1.call-done = f32[4096,256]{0,1:T(8,128)} async-done(((f32[4096,256]{0,1:T(8,128)}), f32[4096,256]{0,1:T(8,128)}) %all-reduce.6.cloned.1.call-update) | async-done | bytes 4194320 | tf_op jit(solution)/shard_map/psum | solution.py:19
  219.1 10.8 %convolution_multiply_fusion.1 = f32[256,256]{0,1:T(8,128)} fusion(f32[4096,256]{0,1:T(8,128)} %all-reduce.6.cloned.1.call-done, f32[4096,256]{1,0:T(8,128)} %param.4), kind=kOutput, calls=%fused_computation.15 | convolution fusion | flops 3221291008 | bytes 8650752 | tf_op jit(solution)/shard_map/dot_general | solution.py:42
  230.2 5.6 copy.9
  235.8 97.1 %all-reduce.8.cloned.1.call-done = f32[256,256]{0,1:T(8,128)} async-done(((f32[256,256]{0,1:T(8,128)}), f32[256,256]{0,1:T(8,128)}) %all-reduce.8.cloned.1.call-update) | async-done | bytes 262160 | tf_op jit(solution)/shard_map/psum | solution.py:52
  332.9 8.1 %convolution_subtract_fusion.1 = f32[4096,256]{0,1:T(8,128)S(1)} fusion(f32[4096,256]{0,1:T(8,128)} %copy.9, f32[4096,256]{0,1:T(8,128)} %all-reduce.6.cloned.1.call-done, f32[256,256]{0,1:T(8,128)} %all-reduce.8.cloned.1.call-done), kind=kOutput, calls=%fused_computation.9 | convolution fusion | flops 3222274048 | bytes 12845056 | tf_op jit(solution)/shard_map/dot_general | solution.py:53
  341.1 3.9 fusion.4
  344.9 0.8 collective-permute-start.5
  345.7 1.2 collective-permute-done.5
  347.4 7.1 %collective-permute-done.6 = f32[256,256]{0,1:T(8,128)S(1)} collective-permute-done((f32[256,256]{0,1:T(8,128)S(1)}, f32[256,256]{0,1:T(8,128)S(1)}, u32[]{:S(2)}, u32[]{:S(2)}) %collective-permute-start.6) | collective-permute-done | bytes 262176 | tf_op jit(solution)/shard_map/ppermute | solution.py:14
  354.5 2.6 collective-permute-start.7
  357.1 5.6 collective-permute-done.7
  363.5 5.1 collective-permute-done.8
  368.6 3.4 collective-permute-start.9
  372.0 5.0 collective-permute-done.9
  377.2 11.7 %cholesky.164 = f32[128,128]{1,0:T(8,128)S(1)} custom-call(f32[128,128]{1,0:T(8,128)S(1)} %cholesky.197), custom_call_target="Cholesky" | custom-call | tf_op jit(solution)/shard_map/jit(cholesky)/cholesky | solution.py:31
  389.0 9.8 %custom-call.15 = f32[1,128,128]{1,2,0:T(8,128)S(1)} custom-call(f32[1,128,128]{2,1,0:T(8,128)S(1)} %get-tuple-element.45), custom_call_target="InvertDiagBlocksLowerTriangular" | custom-call | tf_op jit(solution)/shard_map/jit(cholesky)/cholesky | solution.py:31
  400.1 11.7 %cholesky.181 = f32[128,128]{1,0:T(8,128)S(1)} custom-call(f32[128,128]{1,0:T(8,128)S(1)} %slice_subtract_fusion), custom_call_target="Cholesky" | custom-call | tf_op jit(solution)/shard_map/jit(cholesky)/cholesky | solution.py:31
  413.9 4.2 while.5
  414.7 1.4 bitcast_dynamic-update-slice_fusion.5
  416.7 1.4 bitcast_dynamic-update-slice_fusion.5
  418.1 19.7 %custom-call.16 = f32[2,128,128]{1,2,0:T(8,128)S(1)} custom-call(f32[2,128,128]{2,1,0:T(8,128)S(1)} %get-tuple-element.19), custom_call_target="InvertDiagBlocksLowerTriangular" | custom-call | tf_op jit(solution)/shard_map/triangular_solve/custom-call.0 | solution.py:33
  438.7 8.7 %convolution_select_fusion = f32[4096,256]{0,1:T(8,128)} fusion(pred[]{:T(512)S(6)} %eq.20, f32[4096,256]{0,1:T(8,128)} %copy.9, f32[4096,256]{0,1:T(8,128)} %copy-done, pred[]{:T(512)S(6)} %eq.8, f32[128,256]{1,0:T(8,128)S(1)} %fusion.23, f32[128,256]{1,0:T(8,128)S(1)} %fusion.18), kind=kOutput, calls=%fused_computation.4 | convolution fusion | flops 3223388160 | bytes 12845058 | tf_op jit(solution)/shard_map/dot_general | solution.py:34
  447.5 94.0 %all-reduce.10.cloned.1.call-done = f32[4096,256]{0,1:T(8,128)} async-done(((f32[4096,256]{0,1:T(8,128)}), f32[4096,256]{0,1:T(8,128)}) %all-reduce.10.cloned.1.call-update) | async-done | bytes 4194320 | tf_op jit(solution)/shard_map/psum | solution.py:19
  541.5 7.7 %convolution_multiply_fusion = f32[256,256]{0,1:T(8,128)} fusion(f32[4096,256]{0,1:T(8,128)} %all-reduce.10.cloned.1.call-done, f32[4096,256]{0,1:T(8,128)} %copy-done), kind=kOutput, calls=%fused_computation.14 | convolution fusion | flops 3221291008 | bytes 8650752 | tf_op jit(solution)/shard_map/dot_general | solution.py:42
  549.3 102.9 %all-reduce.12.cloned.1.call-done = f32[256,256]{0,1:T(8,128)} async-done(((f32[256,256]{0,1:T(8,128)}), f32[256,256]{0,1:T(8,128)}) %all-reduce.12.cloned.1.call-update) | async-done | bytes 262160 | tf_op jit(solution)/shard_map/psum | solution.py:57
  652.2 1.0 fusion.11
  653.3 1.0 copy.17
  654.3 11.1 %fusion.2 = f32[4096,256]{0,1:T(8,128)} fusion(f32[4096,256]{0,1:T(8,128)} %all-reduce.6.cloned.1.call-done, f32[4096,256]{0,1:T(8,128)} %all-reduce.10.cloned.1.call-done, f32[4096,256]{0,1:T(8,128)} %copy-done, f32[256,256]{0,1:T(8,128)} %all-reduce.12.cloned.1.call-done, pred[]{:T(512)S(6)} %eq.20, pred[]{:T(512)S(6)} %eq.8), kind=kOutput, calls=%fused_computation.10 | convolution fusion | flops 3224371200 | bytes 17039362 | tf_op jit(solution)/shard_map/dot_general | solution.py:58
  665.4 5.6 copy.16
  (72 shorter events, 10.2 us)
Async XLA Ops:
  7.2 212.0 %all-reduce.6.cloned.1.call-start = ((), (), s32[]{:S(2)}) async-start(), calls=%async_computation | async-start | bytes 8388608 | tf_op jit(solution)/shard_map/psum | solution.py:19
  17.4 1.9 collective-permute-start
  19.4 8.0 %collective-permute-start.1 = (f32[256,256]{0,1:T(8,128)S(1)}, f32[256,256]{0,1:T(8,128)S(1)}, u32[]{:S(2)}, u32[]{:S(2)}) collective-permute-start(f32[256,256]{0,1:T(8,128)S(1)} %add.55), channel_id=1, source_target_pairs={{0,8},{8,0},{4,12},{12,4},{16,24},{24,16},{20,28},{28,20},{32,40},... | collective-permute-start | bytes 786440 | tf_op jit(solution)/shard_map/ppermute | solution.py:14
  27.4 8.7 %collective-permute-start.2 = (f32[256,256]{0,1:T(8,128)S(1)}, f32[256,256]{0,1:T(8,128)S(1)}, u32[]{:S(2)}, u32[]{:S(2)}) collective-permute-start(f32[256,256]{0,1:T(8,128)S(1)} %add.56), channel_id=1, source_target_pairs={{0,16},{16,0},{4,20},{20,4},{8,24},{24,8},{12,28},{28,12},{32,48},... | collective-permute-start | bytes 786440 | tf_op jit(solution)/shard_map/ppermute | solution.py:14
  36.2 6.1 collective-permute-start.3
  42.3 7.0 %collective-permute-start.4 = (f32[256,256]{0,1:T(8,128)S(1)}, f32[256,256]{0,1:T(8,128)S(1)}, u32[]{:S(2)}, u32[]{:S(2)}) collective-permute-start(f32[256,256]{0,1:T(8,128)S(1)} %add.58), channel_id=1, source_target_pairs={{0,64},{64,0},{4,68},{68,4},{8,72},{72,8},{12,76},{76,12},{16,80},... | collective-permute-start | bytes 786440 | tf_op jit(solution)/shard_map/ppermute | solution.py:14
  123.1 209.9 %all-reduce.8.cloned.1.call-start = ((), (), s32[]{:S(2)}) async-start(), calls=%async_computation.1 | async-start | bytes 524288 | tf_op jit(solution)/shard_map/psum | solution.py:52
  230.0 311.6 %all-reduce.10.cloned.1.call-start = ((), (), s32[]{:S(2)}) async-start(), calls=%async_computation.2 | async-start | bytes 8388608 | tf_op jit(solution)/shard_map/psum | solution.py:19
  332.9 8.1 %copy-start.1 = (f32[4096,256]{0,1:T(8,128)S(1)}, f32[4096,256]{0,1:T(8,128)}, u32[]{:S(2)}) copy-start(f32[4096,256]{0,1:T(8,128)} %copy.9) | copy-start | bytes 12582916
  341.0 3.9 copy-start
  344.9 1.9 collective-permute-start.5
  346.9 7.6 %collective-permute-start.6 = (f32[256,256]{0,1:T(8,128)S(1)}, f32[256,256]{0,1:T(8,128)S(1)}, u32[]{:S(2)}, u32[]{:S(2)}) collective-permute-start(f32[256,256]{0,1:T(8,128)S(1)} %add.60), channel_id=1, source_target_pairs={{0,8},{8,0},{4,12},{12,4},{16,24},{24,16},{20,28},{28,20},{32,40},... | collective-permute-start | bytes 786440 | tf_op jit(solution)/shard_map/ppermute | solution.py:14
  354.5 8.2 %collective-permute-start.7 = (f32[256,256]{0,1:T(8,128)S(1)}, f32[256,256]{0,1:T(8,128)S(1)}, u32[]{:S(2)}, u32[]{:S(2)}) collective-permute-start(f32[256,256]{0,1:T(8,128)S(1)} %add.61), channel_id=1, source_target_pairs={{0,16},{16,0},{4,20},{20,4},{8,24},{24,8},{12,28},{28,12},{32,48},... | collective-permute-start | bytes 786440 | tf_op jit(solution)/shard_map/ppermute | solution.py:14
  362.8 5.8 collective-permute-start.8
  368.6 8.4 %collective-permute-start.9 = (f32[256,256]{0,1:T(8,128)S(1)}, f32[256,256]{0,1:T(8,128)S(1)}, u32[]{:S(2)}, u32[]{:S(2)}) collective-permute-start(f32[256,256]{0,1:T(8,128)S(1)} %add.63), channel_id=1, source_target_pairs={{0,64},{64,0},{4,68},{68,4},{8,72},{72,8},{12,76},{76,12},{16,80},... | collective-permute-start | bytes 786440 | tf_op jit(solution)/shard_map/ppermute | solution.py:14
  447.4 101.8 %copy-start.2 = (f32[256,256]{0,1:T(8,128)S(1)}, f32[256,256]{0,1:T(8,128)}, u32[]{:S(2)}) copy-start(f32[256,256]{0,1:T(8,128)} %all-reduce.8.cloned.1.call-done) | copy-start | bytes 786436
  447.4 204.8 %all-reduce.12.cloned.1.call-start = ((), (), s32[]{:S(2)}) async-start(), calls=%async_computation.3 | async-start | bytes 524288 | tf_op jit(solution)/shard_map/psum | solution.py:57
Sparse Core Ops, SparseCore 0:
  123.2 95.8 all-reduce.5
  230.1 102.8 all-reduce.7
  447.5 93.9 all-reduce.9
  549.4 102.8 all-reduce.11
where the time goes:
time: 685 us; the launch traced here: 678 us
  waiting for transfers between devices  436 us (64%)
  other arithmetic  110 us (16%)
  matrix products  75.6 us (11%)
  local copies, waits for them, and re-layouts  20.8 us (3%)
  starting transfers between devices  18.3 us (3%)
  between operations  17.2 us (3%)
    psum x2, waiting for transfers between devices, from_root(): return lax.psum(kept, axis)  190 us
    psum x1, waiting for transfers between devices, on_device(): coeff2 = lax.psum(inner_products(basis2, rest1, total_rows), 'row')  103 us
    psum x1, waiting for transfers between devices, on_device(): coeff1 = lax.psum(inner_products(basis1, influence, total_rows), 'row')  97.1 us
    another operation x13, other arithmetic, factor_panel(): lower = jnp.linalg.cholesky(gram)  68.6 us
    ppermute x10, waiting for transfers between devices, partner_2(): return lax.ppermute(block, axis, route)  45.6 us
    another operation x5, other arithmetic, factor_panel(): lax.linalg.triangular_solve(lower, eye, left_side=True, lower=True)  39.4 us
    dot_general x2, matrix products, factor_panel(): lax.dot_general(block, inverse, (((1,), (1,)), ((), ())), precision=lax.P...  20.9 us
    dot_general x2, matrix products, inner_products(): lax.dot_general(basis, block, (((0,), (0,)), ((), ())), precision=lax.Pre...  18.5 us
  transfers between devices with their start and end apart: 14, of which 14 were waited for; matrix products, arithmetic and copies ran while one was open for 1% of the time, Pallas kernels for 0%

commit v1 on v0

v1 whole, which is shorter than its diff:
```python
import functools

import jax
import jax.numpy as jnp
from jax import lax
from jax.experimental import pallas as pl
from jax.experimental.pallas import tpu as pltpu
from jax.sharding import PartitionSpec as P

MESH = pl.DeviceIdType.MESH
F32 = jnp.float32
PANEL = 256
HALF = 128
ROWS = 4096
CHUNK = 128
PIECES = ROWS // CHUNK
EARLY = PIECES // 2
GROUP = 512
APPLY = 256


def mm(a, b, ca=1, cb=0):
    return lax.dot_general(
        a, b, (((ca,), (cb,)), ((), ())),
        precision=lax.Precision.HIGHEST, preferred_element_type=F32,
    )


def spread(v):
    return jnp.broadcast_to(v, (8, HALF))


def eliminate(square, u_ref, li_ref, off, nb=4):
    sub = lax.broadcasted_iota(jnp.int32, (8, HALF), 0)
    lane = lax.broadcasted_iota(jnp.int32, (8, HALF), 1)
    zero = jnp.zeros((8, HALF), F32)
    tiles = HALF // 8
    left = tuple(square[8 * i : 8 * i + 8, :] for i in range(tiles))
    right = tuple(jnp.where(lane == sub + 8 * i, 1.0, 0.0).astype(F32) for i in range(tiles))

    def eight(left, right, q):
        w = [spread(left[0][:, 8 * q + m : 8 * q + m + 1]) for m in range(8)] + [left[0], right[0]]
        rows = [zero, zero]
        for j in range(0, 8, 2):
            pivot = (sub == j) | (sub == j + 1)
            p00, p01, p11 = spread(w[j][j : j + 1]), spread(w[j][j + 1 : j + 2]), spread(w[j + 1][j + 1 : j + 2])
            rd = 1.0 / (p00 * p11 - p01 * p01)
            i00, i01, i11 = p11 * rd, p01 * rd, p00 * rd
            u, v = jnp.where(pivot, 0.0, w[j]), jnp.where(pivot, 0.0, w[j + 1])
            s0 = lax.rsqrt(p00)
            m0 = p01 * (s0 * s0)
            s1 = lax.rsqrt(p11 - m0 * p01)
            for t in list(range(j + 2, 8)) + [8, 9]:
                r0, r1 = spread(w[t][j : j + 1]), spread(w[t][j + 1 : j + 2])
                a, b = r0 * i00 - r1 * i01, r1 * i11 - r0 * i01
                if t >= 8:
                    rows[t - 8] = jnp.where(
                        sub == j, r0 * s0, jnp.where(sub == j + 1, (r1 - m0 * r0) * s1, rows[t - 8])
                    )
                w[t] = jnp.where(sub == j, a, jnp.where(sub == j + 1, b, w[t] - (u * a + v * b)))
        ql = [spread(w[8][m : m + 1]) for m in range(8)]
        qr = [spread(w[9][m : m + 1]) for m in range(8)]

        def total(c, q):
            t = [c[m] * q[m] for m in range(8)]
            return ((t[0] + t[1]) + (t[2] + t[3])) + ((t[4] + t[5]) + (t[6] + t[7]))

        for i in range(1, tiles):
            c = [spread(left[i][:, 8 * q + m : 8 * q + m + 1]) for m in range(8)]
            left[i] = left[i] - total(c, ql)
            right[i] = right[i] - total(c, qr)
        return rows

    def body(b, carry):
        left, right = list(carry[0]), list(carry[1])
        for q in range(nb):
            up, low = eight(left, right, q)
            r = pl.ds(pl.multiple_of(off + 8 * (b * nb + q), 8), 8)
            up = jnp.where(lane >= sub + 8 * q, up, 0.0)
            u_ref[r, off : off + HALF] = pltpu.roll(up, 8 * nb * b, 1)
            li_ref[r, off : off + HALF] = low
            left, right = left[1:] + [zero], right[1:] + [zero]
        left = [pltpu.roll(t, HALF - 8 * nb, 1) for t in left]
        return tuple(left), tuple(right)

    lax.fori_loop(0, tiles // nb, body, (left, right))


def factor(g_ref, u_ref, li_ref, service):
    h, t = slice(0, HALF), slice(HALF, PANEL)
    eliminate(g_ref[h, h], u_ref, li_ref, 0)
    service(2)
    l11 = li_ref[h, h]
    u12 = mm(l11, g_ref[h, t])
    u_ref[h, t] = u12
    u_ref[t, h] = jnp.zeros((HALF, HALF), F32)
    rest = g_ref[t, t] - mm(u12, u12, 0, 0)
    w = mm(u12, l11, 0, 0)
    li_ref[h, t] = jnp.zeros((HALF, HALF), F32)
    eliminate(rest, u_ref, li_ref, HALF)
    li_ref[t, h] = -mm(li_ref[t, t], w)
    service(2)


def kernel(scale, a_hbm, out_hbm, top_ref, bottom_ref,
           own, X, S, out, gown, ge, acc, gl, u1, li1, u2, li2, m1, m2, t1, t2,
           ec, ea, eb, lc, la, lb, ly, lx,
           load_sem, out_sem, xs, xr, ss, sr,
           e_core, e_rs, e_y, e_yr, e_ag, e_agc, l_core, l_rs, l_y, l_yr, l_x, l_ag, l_agc):
    row, y = lax.axis_index("row"), lax.axis_index("col")
    px, pz, k = row // 8, (row // 2) % 4, row % 2
    across, side = (row, 3 - y), (row, y + 1 - 2 * (y % 2))
    other = (row + 1 - 2 * k, y)

    def on_axis(h, c):
        if h == 0:
            return ((c * 4 + pz) * 2 + k, y)
        return ((px * 4 + c) * 2 + k, y)

    first = (px, pz)
    second = (pz, px)

    loads = [
        pltpu.make_async_copy(a_hbm.at[pl.ds(1024 * i, 1024)], own.at[pl.ds(1024 * i, 1024)], load_sem.at[i])
        for i in range(4)
    ]
    for c in loads:
        c.start()
    barrier = pltpu.get_barrier_semaphore()
    partners = [across, side, (row, (y + 2) % 4), other]
    for d in (1, 2, 3):
        partners += [on_axis(0, (px + d) % 4), on_axis(1, (pz + d) % 4)]
    for p in partners:
        pl.semaphore_signal(barrier, inc=1, device_id=p, device_id_type=MESH)
    pl.semaphore_wait(barrier, len(partners))
    for c in loads:
        c.wait()

    def remote(src, dst, send, recv, to):
        return pltpu.make_async_remote_copy(
            src_ref=src, dst_ref=dst, send_sem=send, recv_sem=recv, device_id=to, device_id_type=MESH
        )

    def piece(j):
        return pl.ds(pl.multiple_of(j * CHUNK, CHUNK), CHUNK)

    def to_across(j):
        return remote(own.at[piece(j)], X.at[piece(j)], xs.at[j], xr.at[j], across)

    def to_side(j, src):
        return remote(src.at[piece(j)], S.at[piece(j)], ss.at[j], sr.at[j], side)

    def each(lo, hi, f):
        def step(j, _):
            f(j)
            return 0
        lax.fori_loop(lo, hi, step, 0)

    @pl.when(y == 0)
    def _():
        def go(j):
            to_across(j).start()
            to_side((j + EARLY) % PIECES, own).start()
        each(0, PIECES, go)

    @pl.when(y == 1)
    def _():
        def go(j):
            to_across(j).start()
            to_side(j + EARLY, own).start()
        each(0, EARLY, go)
        each(EARLY, PIECES, lambda j: to_across(j).start())

    @pl.when(y >= 2)
    def _():
        each(EARLY, PIECES, lambda j: to_across(j).start())

    def forward(j):
        to_across(j).wait_recv()
        to_side(j, X).start()

    sent = [0]

    def service(n):
        lo = sent[0]
        hi = min(lo + n, PIECES)
        sent[0] = hi
        if hi > lo:
            pl.when(y >= 2)(lambda: each(lo, hi, forward))

    base = pl.multiple_of(HALF * k, HALF)
    lanes = (slice(0, HALF), slice(HALF, PANEL))

    def rows_a(h, c):
        return pl.ds(pl.multiple_of(base + 32 * c, 32), 32)

    def rows_b(h, c):
        return pl.ds(pl.multiple_of(base + 32 * first[h] + 8 * c, 8), 8)

    def scatter(ref, bc, ba, bb, sem_core, sem_rs, pause):
        n = ref.shape[0]
        c = remote(ref.at[:, pl.ds(pl.multiple_of(HALF * (1 - k), HALF), HALF)], bc, sem_core.at[0], sem_core.at[1], other)
        c.start()
        pause()
        c.wait()
        ref[:, pl.ds(base, HALF), :] += bc[...]
        cs = []
        for h in (0, 1):
            for d in (1, 2, 3):
                to = (first[h] + d) % 4
                cs.append(remote(ref.at[:, rows_a(h, to), lanes[h]], ba.at[h, d - 1],
                                 sem_rs.at[0, 0, h, d - 1], sem_rs.at[0, 1, h, d - 1], on_axis(h, to)))
        for c in cs:
            c.start()
        pause()
        for c in cs:
            c.wait()
        for h in (0, 1):
            r = rows_a(h, first[h])
            ref[:, r, lanes[h]] += (ba[h, 0] + ba[h, 1]) + ba[h, 2]
        cs = []
        for h in (0, 1):
            for d in (1, 2, 3):
                to = (second[h] + d) % 4
                cs.append(remote(ref.at[:, rows_b(h, to), lanes[h]], bb.at[h, d - 1],
                                 sem_rs.at[1, 0, h, d - 1], sem_rs.at[1, 1, h, d - 1], on_axis(1 - h, to)))
        for c in cs:
            c.start()
        pause()
        for c in cs:
            c.wait()
        for h in (0, 1):
            r = rows_b(h, second[h])
            ref[:, r, lanes[h]] += (bb[h, 0] + bb[h, 1]) + bb[h, 2]

    def gather(ref, sem_ag, sem_core, pause):
        for stage, rows, coord in ((0, rows_b, second), (1, rows_a, first)):
            cs = []
            for h in (0, 1):
                r = ref.at[:, rows(h, coord[h]), lanes[h]]
                axis = h if stage == 1 else 1 - h
                for d in (1, 2, 3):
                    cs.append(remote(r, r, sem_ag.at[stage, 0, h, d - 1], sem_ag.at[stage, 1, h, d - 1],
                                     on_axis(axis, (coord[h] + d) % 4)))
            for c in cs:
                c.start()
            pause()
            for c in cs:
                c.wait()
        r = ref.at[:, pl.ds(base, HALF)]
        c = remote(r, r, sem_core.at[0], sem_core.at[1], other)
        c.start()
        pause()
        c.wait()

    def group(g, ref):
        return ref[pl.ds(pl.multiple_of(g * GROUP, GROUP), GROUP), :]

    @pl.when(y < 2)
    def _():
        gown[...] = jnp.zeros_like(gown)
        def go(g):
            b = group(g, own)
            gown[0] += mm(b, b, 0, 0)
        each(0, ROWS // GROUP, go)
        scatter(gown, ec, ea, eb, e_core, e_rs, lambda: None)
        for h in (0, 1):
            r = rows_b(h, second[h])
            ge[y, r, lanes[h]] = gown[0, r, lanes[h]]

    acc[...] = jnp.zeros_like(acc)

    def inner(g):
        o, x, s = group(g, own), group(g, X), group(g, S)

        @pl.when(y == 0)
        def _():
            acc[1] += mm(o, x, 0, 0)
            acc[2] += mm(s, x, 0, 0)

        @pl.when(y == 1)
        def _():
            acc[0] += mm(s, o, 0, 0)
            acc[1] += mm(s, x, 0, 0)
            acc[2] += mm(o, x, 0, 0)

        @pl.when(y == 2)
        def _():
            acc[1] += mm(s, o, 0, 0)
            acc[2] += mm(x, o, 0, 0)

        @pl.when(y == 3)
        def _():
            acc[0] += mm(x, s, 0, 0)
            acc[1] += mm(x, o, 0, 0)
            acc[2] += mm(s, o, 0, 0)

    def arrived(g):
        each(4 * g, 4 * g + 4, lambda j: to_side(j, X).wait_recv())

    service(5)
    pl.when(y >= 2)(lambda: arrived(0))
    pl.when(y >= 2)(lambda: inner(0))
    service(2)

    def to_y(src_y, ref, h, d, send, recv):
        return remote(ref, ref, send, recv, (row, (y + d) % 4))

    shard = [(h, rows_b(h, second[h])) for h in (0, 1)]

    @pl.when(y < 2)
    def _():
        cs = []
        for h, r in shard:
            v = ge.at[y, r, lanes[h]]
            for d in (1, 2, 3):
                cs.append(remote(v, v, e_y.at[h, d - 1], e_yr.at[y, h], (row, (y + d) % 4)))
        for c in cs:
            c.start()
        for c in cs:
            c.wait_send()

    for src in (0, 1):
        @pl.when(y != src)
        def _():
            for h, r in shard:
                v = ge.at[src, r, lanes[h]]
                remote(v, v, e_y.at[h, 0], e_yr.at[src, h], (row, src)).wait_recv()

    gather(ge, e_ag, e_agc, lambda: service(1))
    pl.when(y >= 2)(lambda: arrived(1))
    pl.when(y >= 2)(lambda: inner(1))
    ge[...] = ge[...] * scale
    factor(ge.at[0], u1, li1, service)

    service(EARLY - sent[0])

    @pl.when(y < 2)
    def _():
        def go(g):
            def got(j):
                to_across(j).wait_recv()
                to_side(j, own).wait_recv()
            each(4 * g, 4 * g + 4, got)
            inner(g)
        each(4, 8, go)

    @pl.when(y >= 2)
    def _():
        def go(g):
            arrived(g)
            inner(g)
        each(2, 4, go)

    scatter(acc, lc, la, lb, l_core, l_rs, lambda: service(1))
    cs = []
    for h, r in shard:
        cs.append(remote(acc.at[pl.ds(1, 2), r, lanes[h]], lx.at[h], l_x.at[0, h], l_x.at[1, h], across))
    for c in cs:
        c.start()
    for h, r in shard:
        t1[r, lanes[h]] = acc[0, r, lanes[h]]

    @pl.when(y % 2 == 1)
    def _():
        es = []
        for h, r in shard:
            v = t1.at[r, lanes[h]]
            for d in (1, 2, 3):
                es.append(remote(v, ly.at[y // 2, h], l_y.at[h, d - 1], l_yr.at[y // 2, h], (row, (y + d) % 4)))
        for c in es:
            c.start()
        for c in es:
            c.wait_send()
        for h, r in shard:
            ly[y // 2, h] = t1[r, lanes[h]]

    service(1)
    for src in (1, 3):
        @pl.when(y != src)
        def _():
            for h, r in shard:
                remote(t1.at[r, lanes[h]], ly.at[src // 2, h], l_y.at[h, 0], l_yr.at[src // 2, h], (row, src)).wait_recv()
    for c in cs:
        c.wait()
    for h, r in shard:
        gl[0, r, lanes[h]] = ly[0, h] + ly[1, h]
        gl[1:3, r, lanes[h]] = acc[1:3, r, lanes[h]] + lx[h]
    gather(gl, l_ag, l_agc, lambda: service(1))

    c01 = mm(li1[...], gl[0] * scale)
    t1[...] = c01
    t2[...] = ge[1] - mm(c01, c01, 0, 0)
    service(1)
    factor(t2, u2, li2, service)
    c0j = mm(li1[...], gl[1] * scale)
    c01 = t1[...]
    coeff2 = mm(li2[...], gl[2] * scale - mm(c01, c0j, 0, 0))
    zero = jnp.zeros((PANEL, PANEL), F32)

    @pl.when(y == 0)
    def _():
        top_ref[...] = u1[...]
        bottom_ref[...] = zero
        m1[...] = li1[...].T

    @pl.when(y == 1)
    def _():
        top_ref[...] = t1[...]
        bottom_ref[...] = u2[...]
        m1[...] = li2[...].T
        m2[...] = mm(mm(li1[...], t1[...], 0, 0), li2[...], 1, 1)

    @pl.when(y >= 2)
    def _():
        top_ref[...] = c0j
        bottom_ref[...] = coeff2
        zz = mm(li2[...], coeff2, 0, 0)
        yy = mm(li1[...], c0j - mm(c01, zz), 0, 0)

        @pl.when(y == 2)
        def _():
            m1[...] = zz
            m2[...] = yy

        @pl.when(y == 3)
        def _():
            m1[...] = yy
            m2[...] = zz

    per = APPLY // CHUNK
    steps = ROWS // APPLY

    def part(g):
        return pl.ds(pl.multiple_of(g * APPLY, APPLY), APPLY)

    def store(g):
        return pltpu.make_async_copy(out.at[part(g)], out_hbm.at[part(g)], out_sem.at[g])

    @pl.when(y == 0)
    def _():
        def go(g):
            out[part(g), :] = mm(own[part(g), :], m1[...])
            store(g).start()
        each(0, steps, go)

    @pl.when(y == 1)
    def _():
        def go(i):
            g = (i + steps // 2) % steps
            pl.when(g < steps // 2)(lambda: each(per * g, per * g + per, lambda j: to_side(j, own).wait_recv()))
            out[part(g), :] = mm(own[part(g), :], m1[...]) - mm(S[part(g), :], m2[...])
            store(g).start()
        each(0, steps, go)

    done = sent[0]

    @pl.when(y >= 2)
    def _():
        def reach(g):
            return jnp.minimum(jnp.maximum(done + g // 3, per * g + per), PIECES)
        def go(g):
            each(jnp.where(g == 0, done, reach(g - 1)), reach(g), forward)
            pl.when(g >= steps // 2)(lambda: each(per * g, per * g + per, lambda j: to_side(j, X).wait_recv()))
            out[part(g), :] = (own[part(g), :] - mm(X[part(g), :], m1[...])) - mm(S[part(g), :], m2[...])
            store(g).start()
        each(0, steps, go)

    @pl.when(y < 2)
    def _():
        each(0, EARLY, lambda j: to_across(j).wait_send())

    @pl.when(y != 1)
    def _():
        each(0, EARLY, lambda j: to_side(j, own).wait_send())

    def late(j):
        to_across(j).wait_send()
        to_side(j, own).wait_send()
    each(EARLY, PIECES, late)
    each(0, steps, lambda g: store(g).wait())


def on_device(total_rows, influence):
    vmem = lambda *s: pltpu.VMEM(s, F32)
    dma = lambda *s: pltpu.SemaphoreType.DMA(s)
    square = jax.ShapeDtypeStruct((PANEL, PANEL), F32)
    block = vmem(PANEL, PANEL)
    factored, top, bottom = pl.pallas_call(
        functools.partial(kernel, 1.0 / total_rows),
        name="factor_panels",
        out_shape=[jax.ShapeDtypeStruct((ROWS, PANEL), F32), square, square],
        in_specs=[pl.BlockSpec(memory_space=pl.ANY)],
        out_specs=[pl.BlockSpec(memory_space=pl.ANY)] + [pl.BlockSpec(memory_space=pltpu.VMEM)] * 2,
        scratch_shapes=[
            vmem(ROWS, PANEL), vmem(ROWS, PANEL), vmem(ROWS, PANEL), vmem(ROWS, PANEL),
            vmem(1, PANEL, PANEL), vmem(2, PANEL, PANEL), vmem(3, PANEL, PANEL), vmem(3, PANEL, PANEL),
            block, block, block, block, block, block, block, block,
            vmem(1, HALF, PANEL), vmem(2, 3, 1, 32, HALF), vmem(2, 3, 1, 8, HALF),
            vmem(3, HALF, PANEL), vmem(2, 3, 3, 32, HALF), vmem(2, 3, 3, 8, HALF),
            vmem(2, 2, 8, HALF), vmem(2, 2, 8, HALF),
            dma(4), dma(ROWS // APPLY), dma(PIECES), dma(PIECES), dma(PIECES), dma(PIECES),
            dma(2), dma(2, 2, 2, 3), dma(2, 3), dma(2, 2), dma(2, 2, 2, 3), dma(2),
            dma(2), dma(2, 2, 2, 3), dma(2, 3), dma(2, 2), dma(2, 2), dma(2, 2, 2, 3), dma(2),
        ],
        compiler_params=pltpu.CompilerParams(
            collective_id=0, has_side_effects=True, vmem_limit_bytes=56 * 2**20
        ),
    )(influence)
    return factored, jnp.concatenate([top, bottom], axis=0)


def solution(mesh):
    total_rows = ROWS * mesh.shape["row"]
    return jax.shard_map(
        functools.partial(on_device, total_rows),
        mesh=mesh,
        in_specs=(P("row", "col"),),
        out_specs=(P("row", "col"), P(None, "col")),
        check_vma=False,
    )
```

time: 685 us -> 197 us (0.29)
  waiting for transfers between devices: 436 us -> 0 us
  Pallas kernels: 0 us -> 189 us
  other arithmetic: 110 us -> 1.86 us
  matrix products: 75.6 us -> 0 us
  starting transfers between devices: 18.3 us -> 0 us
  between operations: 17.2 us -> 0.64 us
  local copies, waits for them, and re-layouts: 20.8 us -> 4.47 us
    psum x4 -> x0, waiting for transfers between devices: 390 us -> none  [the longest x2 190 us: from_root(): return lax.psum(kept, axis)]
    pallas_call x0 -> x1, Pallas kernels: none -> 189 us  [on_device(): pl.pallas_call(functools.partial(kernel, 1.0 / total_rows), name='factor_...]
    another operation x18 -> x0, other arithmetic: 108 us -> none  [the longest x13 68.6 us: factor_panel(): lower = jnp.linalg.cholesky(gram)]
    dot_general x8 -> x0, matrix products: 72.7 us -> none  [the longest x2 20.9 us: factor_panel(): lax.dot_general(block, inverse, (((1,), (1,)), ((), ())), precision=lax.P...]
    ppermute x10 -> x0, waiting for transfers between devices: 45.6 us -> none  [partner_2(): return lax.ppermute(block, axis, route)]
    ppermute x10 -> x0, starting transfers between devices: 18 us -> none  [partner_2(): return lax.ppermute(block, axis, route)]
    another operation x23 -> x0, local copies, waits for them, and re-layouts: 8.3 us -> none  [the longest x15 8.06 us: factor_panel(): lax.linalg.triangular_solve(lower, eye, left_side=True, lower=True)]
    unnamed x9 -> x1, local copies, waits for them, and re-layouts: 12.2 us -> 4.47 us
  transfers between devices with their start and end apart: 14 -> 0, of which waited for: 14 -> 0; matrix products, arithmetic and copies ran while one was open for 1% -> 0% of each run, Pallas kernels for 0% -> 0%
where the time goes in v1:
time: 197 us; the launch traced here: 196 us
  Pallas kernels  189 us (96%)
  local copies, waits for them, and re-layouts  4.47 us (2%)
    pallas_call x1, Pallas kernels, on_device(): pl.pallas_call(functools.partial(kernel, 1.0 / total_rows), name='factor_...  189 us
    unnamed x1, local copies, waits for them, and re-layouts  4.47 us

profile of v1, /device:TPU:17, one launch (start us, length us, event | category | flops | bytes accessed | tf_op | source)
XLA Modules:
  0.0 196.1 jit_solution(5271248683874440192)
XLA Ops:
  0.6 189.1 %factor_panels.1 = (f32[4096,256]{1,0:T(8,128)}, f32[256,256]{1,0:T(8,128)}, f32[256,256]{1,0:T(8,128)}) custom-call(f32[4096,256]{1,0:T(8,128)} %a_hbm.1), custom_call_target="tpu_custom_call" | custom-call | tf_op jit(solution)/shard_map/factor_panels/pallas_call | solution.py:489
  189.8 1.9 pad_maximum_fusion
  191.6 4.5 %copy.4 = f32[4096,256]{1,0:T(8,128)} copy(f32[4096,256]{1,0:T(8,128)} %get-tuple-element.10) | data formatting | bytes 8388608

commit v2 on v1

--- a/solution.py
+++ b/solution.py
@@ -15,7 +15,8 @@
 CHUNK = 128
 PIECES = ROWS // CHUNK
 EARLY = PIECES // 2
-GROUP = 512
+GROUP = 256
+LAG = 3
 APPLY = 256
 
 
@@ -30,7 +31,7 @@
     return jnp.broadcast_to(v, (8, HALF))
 
 
-def eliminate(square, u_ref, li_ref, off, nb=4):
+def eliminate(square, u_ref, li_ref, hook, nb=4):
     sub = lax.broadcasted_iota(jnp.int32, (8, HALF), 0)
     lane = lax.broadcasted_iota(jnp.int32, (8, HALF), 1)
     zero = jnp.zeros((8, HALF), F32)
@@ -75,35 +76,47 @@
         left, right = list(carry[0]), list(carry[1])
         for q in range(nb):
             up, low = eight(left, right, q)
-            r = pl.ds(pl.multiple_of(off + 8 * (b * nb + q), 8), 8)
+            r = pl.ds(pl.multiple_of(8 * (b * nb + q), 8), 8)
             up = jnp.where(lane >= sub + 8 * q, up, 0.0)
-            u_ref[r, off : off + HALF] = pltpu.roll(up, 8 * nb * b, 1)
-            li_ref[r, off : off + HALF] = low
+            u_ref[r, :] = pltpu.roll(up, 8 * nb * b, 1)
+            li_ref[r, :] = low
             left, right = left[1:] + [zero], right[1:] + [zero]
         left = [pltpu.roll(t, HALF - 8 * nb, 1) for t in left]
+        hook(b)
         return tuple(left), tuple(right)
 
     lax.fori_loop(0, tiles // nb, body, (left, right))
 
 
-def factor(g_ref, u_ref, li_ref, service):
-    h, t = slice(0, HALF), slice(HALF, PANEL)
-    eliminate(g_ref[h, h], u_ref, li_ref, 0)
-    service(2)
-    l11 = li_ref[h, h]
-    u12 = mm(l11, g_ref[h, t])
-    u_ref[h, t] = u12
-    u_ref[t, h] = jnp.zeros((HALF, HALF), F32)
-    rest = g_ref[t, t] - mm(u12, u12, 0, 0)
-    w = mm(u12, l11, 0, 0)
-    li_ref[h, t] = jnp.zeros((HALF, HALF), F32)
-    eliminate(rest, u_ref, li_ref, HALF)
-    li_ref[t, h] = -mm(li_ref[t, t], w)
-    service(2)
-
-
-def kernel(scale, a_hbm, out_hbm, top_ref, bottom_ref,
-           own, X, S, out, gown, ge, acc, gl, u1, li1, u2, li2, m1, m2, t1, t2,
+HEAD, TAIL = slice(0, HALF), slice(HALF, PANEL)
+
+
+def factor(g_ref, u_ref, li_ref, parts, us, ls, hook):
+    parts[0] = g_ref[HEAD, HEAD]
+
+    def block(p, _):
+        eliminate(parts[p], us.at[p], ls.at[p], functools.partial(hook, p))
+
+        @pl.when(p == 0)
+        def _():
+            l11 = ls[0]
+            u12 = mm(l11, g_ref[HEAD, TAIL])
+            u_ref[HEAD, TAIL] = u12
+            parts[1] = g_ref[TAIL, TAIL] - mm(u12, u12, 0, 0)
+            li_ref[TAIL, HEAD] = mm(u12, l11, 0, 0)
+        return 0
+
+    lax.fori_loop(0, 2, block, 0)
+    li_ref[TAIL, HEAD] = -mm(ls[1], li_ref[TAIL, HEAD])
+    for p, c in ((0, HEAD), (1, TAIL)):
+        u_ref[c, c] = us[p]
+        li_ref[c, c] = ls[p]
+    u_ref[TAIL, HEAD] = jnp.zeros((HALF, HALF), F32)
+    li_ref[HEAD, TAIL] = jnp.zeros((HALF, HALF), F32)
+
+
+def kernel(scale, a_hbm, out_hbm, upper_ref,
+           own, X, S, out, gown, ge, acc, gl, u1, li1, u2, li2, m1, m2, t1, t2, parts, us, ls,
            ec, ea, eb, lc, la, lb, ly, lx,
            load_sem, out_sem, xs, xr, ss, sr,
            e_core, e_rs, e_y, e_yr, e_ag, e_agc, l_core, l_rs, l_y, l_yr, l_x, l_ag, l_agc):
@@ -156,37 +169,60 @@
             return 0
         lax.fori_loop(lo, hi, step, 0)
 
-    @pl.when(y == 0)
-    def _():
-        def go(j):
-            to_across(j).start()
-            to_side((j + EARLY) % PIECES, own).start()
-        each(0, PIECES, go)
-
-    @pl.when(y == 1)
-    def _():
-        def go(j):
-            to_across(j).start()
-            to_side(j + EARLY, own).start()
-        each(0, EARLY, go)
-        each(EARLY, PIECES, lambda j: to_across(j).start())
+    ahead = 3
 
     @pl.when(y >= 2)
     def _():
-        each(EARLY, PIECES, lambda j: to_across(j).start())
+        each(EARLY, EARLY + ahead, lambda j: to_across(j).start())
 
     def forward(j):
         to_across(j).wait_recv()
         to_side(j, X).start()
 
-    sent = [0]
-
-    def service(n):
-        lo = sent[0]
-        hi = min(lo + n, PIECES)
+        @pl.when(j < EARLY - ahead)
+        def _():
+            to_across(EARLY + j).wait_send()
+            to_across(EARLY + ahead + j).start()
+
+    def turned(j):
+        return (j + EARLY) % PIECES
+
+    def sided(j):
+        return (y == 0) | (j < EARLY)
+
+    def old_piece(j):
+        to_across(j).wait_send()
+        pl.when(sided(j))(lambda: to_side(turned(j), own).wait_send())
+
+    def new_piece(j):
+        pl.when(j >= LAG)(lambda: old_piece(j - LAG))
+        to_across(j).start()
+        pl.when(sided(j))(lambda: to_side(turned(j), own).start())
+
+    sent, passed = [0], [0]
+
+    def source(n):
+        lo, hi = sent[0], min(sent[0] + n, PIECES)
         sent[0] = hi
         if hi > lo:
+            pl.when(y < 2)(lambda: each(lo, hi, new_piece))
+
+    def sink(n):
+        lo, hi = passed[0], min(passed[0] + n, PIECES)
+        passed[0] = hi
+        if hi > lo:
             pl.when(y >= 2)(lambda: each(lo, hi, forward))
+
+    def service(n):
+        source(n)
+        sink(n)
+
+    def hooked(lo, past):
+        def hook(p, b):
+            j = 2 * p + b // 2
+            pl.when((b % 2 == 1) & (y < 2) & (lo + j < PIECES))(lambda: new_piece(lo + j))
+            pl.when((b % 2 == 1) & (y >= 2) & (past + j < PIECES))(lambda: forward(past + j))
+        return hook
 
     base = pl.multiple_of(HALF * k, HALF)
     lanes = (slice(0, HALF), slice(HALF, PANEL))
@@ -197,11 +233,11 @@
     def rows_b(h, c):
         return pl.ds(pl.multiple_of(base + 32 * first[h] + 8 * c, 8), 8)
 
-    def scatter(ref, bc, ba, bb, sem_core, sem_rs, pause):
+    def scatter(ref, bc, ba, bb, sem_core, sem_rs, pauses):
         n = ref.shape[0]
         c = remote(ref.at[:, pl.ds(pl.multiple_of(HALF * (1 - k), HALF), HALF)], bc, sem_core.at[0], sem_core.at[1], other)
         c.start()
-        pause()
+        pauses[0]()
         c.wait()
         ref[:, pl.ds(base, HALF), :] += bc[...]
         cs = []
@@ -212,7 +248,7 @@
                                  sem_rs.at[0, 0, h, d - 1], sem_rs.at[0, 1, h, d - 1], on_axis(h, to)))
         for c in cs:
             c.start()
-        pause()
+        pauses[1]()
         for c in cs:
             c.wait()
         for h in (0, 1):
@@ -226,27 +262,29 @@
                                  sem_rs.at[1, 0, h, d - 1], sem_rs.at[1, 1, h, d - 1], on_axis(1 - h, to)))
         for c in cs:
             c.start()
-        pause()
+        pauses[2]()
         for c in cs:
             c.wait()
         for h in (0, 1):
             r = rows_b(h, second[h])
             ref[:, r, lanes[h]] += (bb[h, 0] + bb[h, 1]) + bb[h, 2]
 
-    def gather(ref, sem_ag, sem_core, pause):
-        for stage, rows, coord in ((0, rows_b, second), (1, rows_a, first)):
-            cs = []
-            for h in (0, 1):
-                r = ref.at[:, rows(h, coord[h]), lanes[h]]
-                axis = h if stage == 1 else 1 - h
-                for d in (1, 2, 3):
-                    cs.append(remote(r, r, sem_ag.at[stage, 0, h, d - 1], sem_ag.at[stage, 1, h, d - 1],
-                                     on_axis(axis, (coord[h] + d) % 4)))
-            for c in cs:
-                c.start()
-            pause()
-            for c in cs:
-                c.wait()
+    def gather_axis(ref, sem_ag, stage, pause):
+        rows, coord = ((rows_b, second), (rows_a, first))[stage]
+        cs = []
+        for h in (0, 1):
+            r = ref.at[:, rows(h, coord[h]), lanes[h]]
+            axis = h if stage == 1 else 1 - h
+            for d in (1, 2, 3):
+                cs.append(remote(r, r, sem_ag.at[stage, 0, h, d - 1], sem_ag.at[stage, 1, h, d - 1],
+                                 on_axis(axis, (coord[h] + d) % 4)))
+        for c in cs:
+            c.start()
+        pause()
+        for c in cs:
+            c.wait()
+
+    def gather_core(ref, sem_core, pause):
         r = ref.at[:, pl.ds(base, HALF)]
         c = remote(r, r, sem_core.at[0], sem_core.at[1], other)
         c.start()
@@ -256,14 +294,19 @@
     def group(g, ref):
         return ref[pl.ds(pl.multiple_of(g * GROUP, GROUP), GROUP), :]
 
+    source(3)
+
     @pl.when(y < 2)
     def _():
         gown[...] = jnp.zeros_like(gown)
+
         def go(g):
             b = group(g, own)
             gown[0] += mm(b, b, 0, 0)
+            pl.when(g % 8 == 7)(lambda: new_piece(3 + g // 8))
         each(0, ROWS // GROUP, go)
-        scatter(gown, ec, ea, eb, e_core, e_rs, lambda: None)
+        sent[0] = 5
+        scatter(gown, ec, ea, eb, e_core, e_rs, [lambda: source(1)] * 3)
         for h in (0, 1):
             r = rows_b(h, second[h])
             ge[y, r, lanes[h]] = gown[0, r, lanes[h]]
@@ -271,88 +314,97 @@
     acc[...] = jnp.zeros_like(acc)
 
     def inner(g):
-        o, x, s = group(g, own), group(g, X), group(g, S)
+        def two(a, b, c):
+            both = mm(jnp.concatenate([group(g, a), group(g, b)], axis=1), group(g, c), 0, 0)
+            acc[1] += both[:PANEL]
+            acc[2] += both[PANEL:]
+
+        def one(a, b):
+            acc[0] += mm(group(g, a), group(g, b), 0, 0)
 
         @pl.when(y == 0)
         def _():
-            acc[1] += mm(o, x, 0, 0)
-            acc[2] += mm(s, x, 0, 0)
+            two(own, S, X)
 
         @pl.when(y == 1)
         def _():
-            acc[0] += mm(s, o, 0, 0)
-            acc[1] += mm(s, x, 0, 0)
-            acc[2] += mm(o, x, 0, 0)
+            two(S, own, X)
+            one(S, own)
 
         @pl.when(y == 2)
         def _():
-            acc[1] += mm(s, o, 0, 0)
-            acc[2] += mm(x, o, 0, 0)
+            two(S, X, own)
 
         @pl.when(y == 3)
         def _():
-            acc[0] += mm(x, s, 0, 0)
-            acc[1] += mm(x, o, 0, 0)
-            acc[2] += mm(s, o, 0, 0)
-
-    def arrived(g):
-        each(4 * g, 4 * g + 4, lambda j: to_side(j, X).wait_recv())
-
-    service(5)
-    pl.when(y >= 2)(lambda: arrived(0))
-    pl.when(y >= 2)(lambda: inner(0))
-    service(2)
-
-    def to_y(src_y, ref, h, d, send, recv):
-        return remote(ref, ref, send, recv, (row, (y + d) % 4))
+            two(X, S, own)
+            one(X, S)
 
     shard = [(h, rows_b(h, second[h])) for h in (0, 1)]
 
+    def shard_sends():
+        return [
+            remote(v, v, e_y.at[h, d - 1], e_yr.at[y, h], (row, (y + d) % 4))
+            for h, r in shard for v in [ge.at[y, r, lanes[h]]] for d in (1, 2, 3)
+        ]
+
     @pl.when(y < 2)
     def _():
-        cs = []
-        for h, r in shard:
-            v = ge.at[y, r, lanes[h]]
-            for d in (1, 2, 3):
-                cs.append(remote(v, v, e_y.at[h, d - 1], e_yr.at[y, h], (row, (y + d) % 4)))
-        for c in cs:
+        for c in shard_sends():
             c.start()
-        for c in cs:
-            c.wait_send()
-
-    for src in (0, 1):
-        @pl.when(y != src)
-        def _():
-            for h, r in shard:
-                v = ge.at[src, r, lanes[h]]
-                remote(v, v, e_y.at[h, 0], e_yr.at[src, h], (row, src)).wait_recv()
-
-    gather(ge, e_ag, e_agc, lambda: service(1))
-    pl.when(y >= 2)(lambda: arrived(1))
-    pl.when(y >= 2)(lambda: inner(1))
-    ge[...] = ge[...] * scale
-    factor(ge.at[0], u1, li1, service)
-
-    service(EARLY - sent[0])
-
-    @pl.when(y < 2)
-    def _():
-        def go(g):
+
+    source(1)
+    sink(2)
+    QUARTER = EARLY // 4
+
+    def step(i, _):
+        @pl.when(y < 2)
+        def _():
+            new_piece(jnp.where(i == 3, 18, 9 + 2 * i))
             def got(j):
                 to_across(j).wait_recv()
                 to_side(j, own).wait_recv()
-            each(4 * g, 4 * g + 4, got)
-            inner(g)
-        each(4, 8, go)
-
-    @pl.when(y >= 2)
-    def _():
-        def go(g):
-            arrived(g)
-            inner(g)
-        each(2, 4, go)
-
-    scatter(acc, lc, la, lb, l_core, l_rs, lambda: service(1))
+            each(EARLY + QUARTER * i, EARLY + QUARTER * i + QUARTER, got)
+            each(8 + 2 * i, 10 + 2 * i, inner)
+            pl.when(i < 2)(lambda: new_piece(10 + 2 * i))
+
+        @pl.when(y >= 2)
+        def _():
+            pl.when(i < 3)(lambda: each(4 * i + 2, 4 * i + 4, forward))
+            each(QUARTER * i, QUARTER * i + QUARTER, lambda j: to_side(j, X).wait_recv())
+            each(2 * i, 2 * i + 2, inner)
+            pl.when(i < 2)(lambda: each(4 * i + 4, 4 * i + 6, forward))
+            pl.when(i == 2)(lambda: forward(12))
+
+        @pl.when(i == 0)
+        def _():
+            @pl.when(y < 2)
+            def _():
+                for c in shard_sends():
+                    c.wait_send()
+            for src in (0, 1):
+                @pl.when(y != src)
+                def _():
+                    for h, r in shard:
+                        v = ge.at[src, r, lanes[h]]
+                        remote(v, v, e_y.at[h, 0], e_yr.at[src, h], (row, src)).wait_recv()
+            gather_axis(ge, e_ag, 0, lambda: None)
+
+        @pl.when(i == 1)
+        def _():
+            gather_axis(ge, e_ag, 1, lambda: None)
+            gather_core(ge, e_agc, lambda: None)
+
+        @pl.when(i == 2)
+        def _():
+            ge[...] = ge[...] * scale
+            factor(ge.at[0], u1, li1, parts, us, ls, hooked(14, 13))
+        return 0
+
+    lax.fori_loop(0, 4, step, 0)
+    sent[0], passed[0] = 19, 17
+
+    scatter(acc, lc, la, lb, l_core, l_rs, [lambda: service(1), lambda: service(2), lambda: service(1)])
     cs = []
     for h, r in shard:
         cs.append(remote(acc.at[pl.ds(1, 2), r, lanes[h]], lx.at[h], l_x.at[0, h], l_x.at[1, h], across))
@@ -375,7 +427,7 @@
         for h, r in shard:
             ly[y // 2, h] = t1[r, lanes[h]]
 
-    service(1)
+    service(2)
     for src in (1, 3):
         @pl.when(y != src)
         def _():
@@ -386,13 +438,16 @@
     for h, r in shard:
         gl[0, r, lanes[h]] = ly[0, h] + ly[1, h]
         gl[1:3, r, lanes[h]] = acc[1:3, r, lanes[h]] + lx[h]
-    gather(gl, l_ag, l_agc, lambda: service(1))
+    gather_axis(gl, l_ag, 0, lambda: service(1))
+    gather_axis(gl, l_ag, 1, lambda: service(2))
+    gather_core(gl, l_agc, lambda: service(1))
 
     c01 = mm(li1[...], gl[0] * scale)
     t1[...] = c01
     t2[...] = ge[1] - mm(c01, c01, 0, 0)
-    service(1)
-    factor(t2, u2, li2, service)
+    factor(t2, u2, li2, parts, us, ls, hooked(sent[0], passed[0]))
+    sent[0], passed[0] = min(sent[0] + 4, PIECES), min(passed[0] + 4, PIECES)
+    source(PIECES)
     c0j = mm(li1[...], gl[1] * scale)
     c01 = t1[...]
     coeff2 = mm(li2[...], gl[2] * scale - mm(c01, c0j, 0, 0))
@@ -400,21 +455,21 @@
 
     @pl.when(y == 0)
     def _():
-        top_ref[...] = u1[...]
-        bottom_ref[...] = zero
+        upper_ref[:PANEL] = u1[...]
+        upper_ref[PANEL:] = zero
         m1[...] = li1[...].T
 
     @pl.when(y == 1)
     def _():
-        top_ref[...] = t1[...]
-        bottom_ref[...] = u2[...]
+        upper_ref[:PANEL] = t1[...]
+        upper_ref[PANEL:] = u2[...]
         m1[...] = li2[...].T
         m2[...] = mm(mm(li1[...], t1[...], 0, 0), li2[...], 1, 1)
 
     @pl.when(y >= 2)
     def _():
-        top_ref[...] = c0j
-        bottom_ref[...] = coeff2
+        upper_ref[:PANEL] = c0j
+        upper_ref[PANEL:] = coeff2
         zz = mm(li2[...], coeff2, 0, 0)
         yy = mm(li1[...], c0j - mm(c01, zz), 0, 0)
 
@@ -453,7 +508,7 @@
             store(g).start()
         each(0, steps, go)
 
-    done = sent[0]
+    done = passed[0]
 
     @pl.when(y >= 2)
     def _():
@@ -468,34 +523,31 @@
 
     @pl.when(y < 2)
     def _():
-        each(0, EARLY, lambda j: to_across(j).wait_send())
-
-    @pl.when(y != 1)
-    def _():
-        each(0, EARLY, lambda j: to_side(j, own).wait_send())
-
-    def late(j):
-        to_across(j).wait_send()
-        to_side(j, own).wait_send()
-    each(EARLY, PIECES, late)
+        each(PIECES - LAG, PIECES, old_piece)
+
+    @pl.when(y >= 2)
+    def _():
+        each(PIECES - ahead, PIECES, lambda j: to_across(j).wait_send())
+        each(0, PIECES, lambda j: to_side(j, X).wait_send())
+
     each(0, steps, lambda g: store(g).wait())
 
 
 def on_device(total_rows, influence):
     vmem = lambda *s: pltpu.VMEM(s, F32)
     dma = lambda *s: pltpu.SemaphoreType.DMA(s)
-    square = jax.ShapeDtypeStruct((PANEL, PANEL), F32)
     block = vmem(PANEL, PANEL)
-    factored, top, bottom = pl.pallas_call(
+    factored, upper = pl.pallas_call(
         functools.partial(kernel, 1.0 / total_rows),
         name="factor_panels",
-        out_shape=[jax.ShapeDtypeStruct((ROWS, PANEL), F32), square, square],
+        out_shape=[jax.ShapeDtypeStruct((ROWS, PANEL), F32), jax.ShapeDtypeStruct((2 * PANEL, PANEL), F32)],
         in_specs=[pl.BlockSpec(memory_space=pl.ANY)],
-        out_specs=[pl.BlockSpec(memory_space=pl.ANY)] + [pl.BlockSpec(memory_space=pltpu.VMEM)] * 2,
+        out_specs=[pl.BlockSpec(memory_space=pl.ANY)] + [pl.BlockSpec(memory_space=pltpu.VMEM)],
         scratch_shapes=[
             vmem(ROWS, PANEL), vmem(ROWS, PANEL), vmem(ROWS, PANEL), vmem(ROWS, PANEL),
             vmem(1, PANEL, PANEL), vmem(2, PANEL, PANEL), vmem(3, PANEL, PANEL), vmem(3, PANEL, PANEL),
             block, block, block, block, block, block, block, block,
+            vmem(2, HALF, HALF), vmem(2, HALF, HALF), vmem(2, HALF, HALF),
             vmem(1, HALF, PANEL), vmem(2, 3, 1, 32, HALF), vmem(2, 3, 1, 8, HALF),
             vmem(3, HALF, PANEL), vmem(2, 3, 3, 32, HALF), vmem(2, 3, 3, 8, HALF),
             vmem(2, 2, 8, HALF), vmem(2, 2, 8, HALF),
@@ -507,7 +559,7 @@
             collective_id=0, has_side_effects=True, vmem_limit_bytes=56 * 2**20
         ),
     )(influence)
-    return factored, jnp.concatenate([top, bottom], axis=0)
+    return factored, upper
 
 
 def solution(mesh):

time: 197 us -> 131 us (0.66)
  Pallas kernels: 189 us -> 124 us
    pallas_call x1, Pallas kernels: 189 us -> 124 us  [on_device(): pl.pallas_call(functools.partial(kernel, 1.0 / total_rows), name='factor_...]
    unnamed x1 -> x4, local copies, waits for them, and re-layouts: 4.47 us -> 5.33 us
where the time goes in v2:
time: 131 us; the launch traced here: 130 us
  Pallas kernels  124 us (95%)
  local copies, waits for them, and re-layouts  5.33 us (4%)
    pallas_call x1, Pallas kernels, on_device(): pl.pallas_call(functools.partial(kernel, 1.0 / total_rows), name='factor_...  124 us
    unnamed x4, local copies, waits for them, and re-layouts  5.33 us

profile of v2, /device:TPU:17, one launch (start us, length us, event | category | flops | bytes accessed | tf_op | source)
XLA Modules:
  0.0 129.9 jit_solution(3752616051105486965)
XLA Ops:
  0.6 123.9 %factor_panels.1 = (f32[4096,256]{1,0:T(8,128)}, f32[512,256]{1,0:T(8,128)}) custom-call(f32[4096,256]{1,0:T(8,128)} %a_hbm.1), custom_call_target="tpu_custom_call" | custom-call | tf_op jit(solution)/shard_map/factor_panels/pallas_call | solution.py:540
  124.5 0.0 copy-start
  124.5 4.5 %copy.5 = f32[4096,256]{1,0:T(8,128)} copy(f32[4096,256]{1,0:T(8,128)} %get-tuple-element.4) | data formatting | bytes 8388608
  129.1 0.0 copy-done
  129.1 0.8 copy.6
Async XLA Ops:
  124.5 4.5 %copy-start = (f32[512,256]{1,0:T(8,128)S(1)}, f32[512,256]{1,0:T(8,128)}, u32[]{:S(2)}) copy-start(f32[512,256]{1,0:T(8,128)} %get-tuple-element.5) | copy-start | bytes 1572868

commit v3 on v2

--- a/solution.py
+++ b/solution.py
@@ -16,8 +16,9 @@
 PIECES = ROWS // CHUNK
 EARLY = PIECES // 2
 GROUP = 256
-LAG = 3
-APPLY = 256
+EXTRA = 1
+LAG = 6
+APPLY = 512
 
 
 def mm(a, b, ca=1, cb=0):
@@ -25,6 +26,21 @@
         a, b, (((ca,), (cb,)), ((), ())),
         precision=lax.Precision.HIGHEST, preferred_element_type=F32,
     )
+
+
+BF16 = jnp.bfloat16
+TERMS = ((2, 0), (0, 2), (1, 1), (1, 0), (0, 1), (0, 0))
+
+
+def three(a):
+    high = a.astype(BF16)
+    rest = a - high.astype(F32)
+    middle = rest.astype(BF16)
+    return high, middle, (rest - middle.astype(F32)).astype(BF16)
+
+
+def stacked(parts_of, side, axis):
+    return jnp.concatenate([p[t[side]] for t in TERMS for p in parts_of], axis=axis)
 
 
 def spread(v):
@@ -116,22 +132,27 @@
 
 
 def kernel(scale, a_hbm, out_hbm, upper_ref,
-           own, X, S, out, gown, ge, acc, gl, u1, li1, u2, li2, m1, m2, t1, t2, parts, us, ls,
+           own, X, S, out, gown, ge, acc, gl, u1, u2, m1, m2, mcat, sq, parts, us, ls,
            ec, ea, eb, lc, la, lb, ly, lx,
            load_sem, out_sem, xs, xr, ss, sr,
-           e_core, e_rs, e_y, e_yr, e_ag, e_agc, l_core, l_rs, l_y, l_yr, l_x, l_ag, l_agc):
+           e_core, e_rs, e_y, e_yr, e_ag, e_agc, l_core, l_rs, l_y, l_yr, l_x, l_ag, l_agc, l_agb, l_agbc):
     row, y = lax.axis_index("row"), lax.axis_index("col")
     px, pz, k = row // 8, (row // 2) % 4, row % 2
+    qx = px + 1 - 2 * (px % 2)
     across, side = (row, 3 - y), (row, y + 1 - 2 * (y % 2))
     other = (row + 1 - 2 * k, y)
 
     def on_axis(h, c):
-        if h == 0:
-            return ((c * 4 + pz) * 2 + k, y)
-        return ((px * 4 + c) * 2 + k, y)
-
-    first = (px, pz)
-    second = (pz, px)
+        return (jnp.where(h == 0, (c * 4 + pz) * 2 + k, (px * 4 + c) * 2 + k), y)
+
+    def beside(d):
+        return ((qx * 4 + pz) * 2 + k, (y + d) % 4)
+
+    def first(h, x=px):
+        return jnp.where(h == 0, x, pz)
+
+    def second(h, x=px):
+        return jnp.where(h == 0, pz, x)
 
     loads = [
         pltpu.make_async_copy(a_hbm.at[pl.ds(1024 * i, 1024)], own.at[pl.ds(1024 * i, 1024)], load_sem.at[i])
@@ -140,7 +161,7 @@
     for c in loads:
         c.start()
     barrier = pltpu.get_barrier_semaphore()
-    partners = [across, side, (row, (y + 2) % 4), other]
+    partners = [across, side, other] + [beside(d) for d in (1, 2, 3)]
     for d in (1, 2, 3):
         partners += [on_axis(0, (px + d) % 4), on_axis(1, (pz + d) % 4)]
     for p in partners:
@@ -169,7 +190,7 @@
             return 0
         lax.fori_loop(lo, hi, step, 0)
 
-    ahead = 3
+    ahead = 8
 
     @pl.when(y >= 2)
     def _():
@@ -225,76 +246,70 @@
         return hook
 
     base = pl.multiple_of(HALF * k, HALF)
-    lanes = (slice(0, HALF), slice(HALF, PANEL))
+
+    def lanes(h):
+        return pl.ds(pl.multiple_of(HALF * h, HALF), HALF)
 
     def rows_a(h, c):
         return pl.ds(pl.multiple_of(base + 32 * c, 32), 32)
 
-    def rows_b(h, c):
-        return pl.ds(pl.multiple_of(base + 32 * first[h] + 8 * c, 8), 8)
+    def rows_b(h, c, x=px):
+        return pl.ds(pl.multiple_of(base + 32 * first(h, x) + 8 * c, 8), 8)
+
+    def exchange(make, n, pause):
+        each(0, n, lambda j: make(j).start())
+        pause()
+        each(0, n, lambda j: make(j).wait())
 
     def scatter(ref, bc, ba, bb, sem_core, sem_rs, pauses):
-        n = ref.shape[0]
-        c = remote(ref.at[:, pl.ds(pl.multiple_of(HALF * (1 - k), HALF), HALF)], bc, sem_core.at[0], sem_core.at[1], other)
-        c.start()
-        pauses[0]()
-        c.wait()
+        def halves(j):
+            away = pl.ds(pl.multiple_of(HALF * (1 - k), HALF), HALF)
+            return remote(ref.at[:, away], bc, sem_core.at[0], sem_core.at[1], other)
+
+        def wide(j):
+            h, d = j // 3, j % 3
+            to = (first(h) + d + 1) % 4
+            return remote(ref.at[:, rows_a(h, to), lanes(h)], ba.at[h, d],
+                          sem_rs.at[0, 0, h, d], sem_rs.at[0, 1, h, d], on_axis(h, to))
+
+        def narrow(j):
+            h, d = j // 3, j % 3
+            to = (second(h) + d + 1) % 4
+            return remote(ref.at[:, rows_b(h, to), lanes(h)], bb.at[h, d],
+                          sem_rs.at[1, 0, h, d], sem_rs.at[1, 1, h, d], on_axis(1 - h, to))
+
+        exchange(halves, 1, pauses[0])
         ref[:, pl.ds(base, HALF), :] += bc[...]
-        cs = []
+        exchange(wide, 6, pauses[1])
         for h in (0, 1):
-            for d in (1, 2, 3):
-                to = (first[h] + d) % 4
-                cs.append(remote(ref.at[:, rows_a(h, to), lanes[h]], ba.at[h, d - 1],
-                                 sem_rs.at[0, 0, h, d - 1], sem_rs.at[0, 1, h, d - 1], on_axis(h, to)))
-        for c in cs:
-            c.start()
-        pauses[1]()
-        for c in cs:
-            c.wait()
+            ref[:, rows_a(h, first(h)), HALF * h : HALF * h + HALF] += (ba[h, 0] + ba[h, 1]) + ba[h, 2]
+        exchange(narrow, 6, pauses[2])
         for h in (0, 1):
-            r = rows_a(h, first[h])
-            ref[:, r, lanes[h]] += (ba[h, 0] + ba[h, 1]) + ba[h, 2]
-        cs = []
-        for h in (0, 1):
-            for d in (1, 2, 3):
-                to = (second[h] + d) % 4
-                cs.append(remote(ref.at[:, rows_b(h, to), lanes[h]], bb.at[h, d - 1],
-                                 sem_rs.at[1, 0, h, d - 1], sem_rs.at[1, 1, h, d - 1], on_axis(1 - h, to)))
-        for c in cs:
-            c.start()
-        pauses[2]()
-        for c in cs:
-            c.wait()
-        for h in (0, 1):
-            r = rows_b(h, second[h])
-            ref[:, r, lanes[h]] += (bb[h, 0] + bb[h, 1]) + bb[h, 2]
-
-    def gather_axis(ref, sem_ag, stage, pause):
-        rows, coord = ((rows_b, second), (rows_a, first))[stage]
-        cs = []
-        for h in (0, 1):
-            r = ref.at[:, rows(h, coord[h]), lanes[h]]
-            axis = h if stage == 1 else 1 - h
-            for d in (1, 2, 3):
-                cs.append(remote(r, r, sem_ag.at[stage, 0, h, d - 1], sem_ag.at[stage, 1, h, d - 1],
-                                 on_axis(axis, (coord[h] + d) % 4)))
-        for c in cs:
-            c.start()
-        pause()
-        for c in cs:
-            c.wait()
-
-    def gather_core(ref, sem_core, pause):
+            ref[:, rows_b(h, second(h)), HALF * h : HALF * h + HALF] += (bb[h, 0] + bb[h, 1]) + bb[h, 2]
+
+    def axis_part(ref, sem_ag, stage):
+        def make(j):
+            h, d = j // 3, j % 3
+            if stage == 0:
+                r, axis, coord = rows_b(h, second(h, qx), qx), 1 - h, second(h)
+            else:
+                r, axis, coord = rows_a(h, first(h, qx)), h, first(h)
+            r = ref.at[:, r, lanes(h)]
+            return remote(r, r, sem_ag.at[stage, 0, h, d], sem_ag.at[stage, 1, h, d],
+                          on_axis(axis, (coord + d + 1) % 4))
+        return make
+
+    def core_part(ref, sem_core):
         r = ref.at[:, pl.ds(base, HALF)]
-        c = remote(r, r, sem_core.at[0], sem_core.at[1], other)
-        c.start()
-        pause()
-        c.wait()
+        return lambda j: remote(r, r, sem_core.at[0], sem_core.at[1], other)
+
+    def mine(h, x=px):
+        return rows_b(h, second(h, x), x), lanes(h)
 
     def group(g, ref):
         return ref[pl.ds(pl.multiple_of(g * GROUP, GROUP), GROUP), :]
 
-    source(3)
+    source(6)
 
     @pl.when(y < 2)
     def _():
@@ -303,13 +318,10 @@
         def go(g):
             b = group(g, own)
             gown[0] += mm(b, b, 0, 0)
-            pl.when(g % 8 == 7)(lambda: new_piece(3 + g // 8))
+            pl.when(g % 8 == 7)(lambda: new_piece(6 + g // 8))
         each(0, ROWS // GROUP, go)
-        sent[0] = 5
+        sent[0] = 8
         scatter(gown, ec, ea, eb, e_core, e_rs, [lambda: source(1)] * 3)
-        for h in (0, 1):
-            r = rows_b(h, second[h])
-            ge[y, r, lanes[h]] = gown[0, r, lanes[h]]
 
     acc[...] = jnp.zeros_like(acc)
 
@@ -340,19 +352,11 @@
             two(X, S, own)
             one(X, S)
 
-    shard = [(h, rows_b(h, second[h])) for h in (0, 1)]
-
-    def shard_sends():
-        return [
-            remote(v, v, e_y.at[h, d - 1], e_yr.at[y, h], (row, (y + d) % 4))
-            for h, r in shard for v in [ge.at[y, r, lanes[h]]] for d in (1, 2, 3)
-        ]
-
-    @pl.when(y < 2)
-    def _():
-        for c in shard_sends():
-            c.start()
-
+    def shard_send(j):
+        h, d = j // 4, j % 4
+        return remote(gown.at[(0, *mine(h))], ge.at[(y, *mine(h))], e_y.at[h, d], e_yr.at[y, h], beside(d))
+
+    pl.when(y < 2)(lambda: each(0, 8, lambda j: shard_send(j).start()))
     source(1)
     sink(2)
     QUARTER = EARLY // 4
@@ -360,17 +364,18 @@
     def step(i, _):
         @pl.when(y < 2)
         def _():
-            new_piece(jnp.where(i == 3, 18, 9 + 2 * i))
+            new_piece(jnp.where(i == 3, 21, 12 + 2 * i))
             def got(j):
                 to_across(j).wait_recv()
                 to_side(j, own).wait_recv()
             each(EARLY + QUARTER * i, EARLY + QUARTER * i + QUARTER, got)
             each(8 + 2 * i, 10 + 2 * i, inner)
-            pl.when(i < 2)(lambda: new_piece(10 + 2 * i))
+            pl.when(i < 2)(lambda: new_piece(13 + 2 * i))
 
         @pl.when(y >= 2)
         def _():
-            pl.when(i < 3)(lambda: each(4 * i + 2, 4 * i + 4, forward))
+            pl.when(i == 0)(lambda: each(2, 4, forward))
+            pl.when(i == 1)(lambda: forward(7))
             each(QUARTER * i, QUARTER * i + QUARTER, lambda j: to_side(j, X).wait_recv())
             each(2 * i, 2 * i + 2, inner)
             pl.when(i < 2)(lambda: each(4 * i + 4, 4 * i + 6, forward))
@@ -378,110 +383,116 @@
 
         @pl.when(i == 0)
         def _():
-            @pl.when(y < 2)
-            def _():
-                for c in shard_sends():
-                    c.wait_send()
-            for src in (0, 1):
-                @pl.when(y != src)
-                def _():
-                    for h, r in shard:
-                        v = ge.at[src, r, lanes[h]]
-                        remote(v, v, e_y.at[h, 0], e_yr.at[src, h], (row, src)).wait_recv()
-            gather_axis(ge, e_ag, 0, lambda: None)
+            pl.when(y < 2)(lambda: each(0, 8, lambda j: shard_send(j).wait_send()))
+
+            def got(j):
+                src, h = j // 2, j % 2
+                v = ge.at[(src, *mine(h, qx))]
+                remote(v, v, e_y.at[h, 0], e_yr.at[src, h], beside(0)).wait_recv()
+            each(0, 4, got)
+            exchange(axis_part(ge, e_ag, 0), 6, lambda: pl.when(y >= 2)(lambda: forward(6)))
 
         @pl.when(i == 1)
         def _():
-            gather_axis(ge, e_ag, 1, lambda: None)
-            gather_core(ge, e_agc, lambda: None)
+            exchange(axis_part(ge, e_ag, 1), 6, lambda: pl.when(y >= 2)(lambda: forward(10)))
+            exchange(core_part(ge, e_agc), 1, lambda: pl.when(y >= 2)(lambda: forward(11)))
 
         @pl.when(i == 2)
         def _():
             ge[...] = ge[...] * scale
-            factor(ge.at[0], u1, li1, parts, us, ls, hooked(14, 13))
+            factor(ge.at[0], u1, sq.at[0], parts, us, ls, hooked(17, 13))
         return 0
 
     lax.fori_loop(0, 4, step, 0)
-    sent[0], passed[0] = 19, 17
+    sent[0], passed[0] = 22, 17
+    sink(EXTRA)
 
     scatter(acc, lc, la, lb, l_core, l_rs, [lambda: service(1), lambda: service(2), lambda: service(1)])
-    cs = []
-    for h, r in shard:
-        cs.append(remote(acc.at[pl.ds(1, 2), r, lanes[h]], lx.at[h], l_x.at[0, h], l_x.at[1, h], across))
-    for c in cs:
-        c.start()
-    for h, r in shard:
-        t1[r, lanes[h]] = acc[0, r, lanes[h]]
-
-    @pl.when(y % 2 == 1)
-    def _():
-        es = []
-        for h, r in shard:
-            v = t1.at[r, lanes[h]]
-            for d in (1, 2, 3):
-                es.append(remote(v, ly.at[y // 2, h], l_y.at[h, d - 1], l_yr.at[y // 2, h], (row, (y + d) % 4)))
-        for c in es:
-            c.start()
-        for c in es:
-            c.wait_send()
-        for h, r in shard:
-            ly[y // 2, h] = t1[r, lanes[h]]
-
+    def swap(j):
+        h, far = j // 2, j % 2
+        r, c = mine(h)
+        to = ((qx * 4 + pz) * 2 + k, jnp.where(far == 1, 3 - y, y))
+        return remote(acc.at[pl.ds(1, 2), r, c], lx.at[far, h], l_x.at[0, far, h], l_x.at[1, far, h], to)
+
+    def first_send(j):
+        h, d = j // 4, j % 4
+        return remote(acc.at[(0, *mine(h))], ly.at[y // 2, h], l_y.at[h, d], l_yr.at[y // 2, h], beside(d))
+
+    pl.when(y % 2 == 1)(lambda: each(0, 8, lambda j: first_send(j).start()))
+    each(0, 4, lambda j: swap(j).start())
     service(2)
-    for src in (1, 3):
-        @pl.when(y != src)
-        def _():
-            for h, r in shard:
-                remote(t1.at[r, lanes[h]], ly.at[src // 2, h], l_y.at[h, 0], l_yr.at[src // 2, h], (row, src)).wait_recv()
-    for c in cs:
-        c.wait()
-    for h, r in shard:
-        gl[0, r, lanes[h]] = ly[0, h] + ly[1, h]
-        gl[1:3, r, lanes[h]] = acc[1:3, r, lanes[h]] + lx[h]
-    gather_axis(gl, l_ag, 0, lambda: service(1))
-    gather_axis(gl, l_ag, 1, lambda: service(2))
-    gather_core(gl, l_agc, lambda: service(1))
-
-    c01 = mm(li1[...], gl[0] * scale)
-    t1[...] = c01
-    t2[...] = ge[1] - mm(c01, c01, 0, 0)
-    factor(t2, u2, li2, parts, us, ls, hooked(sent[0], passed[0]))
+
+    def got_first(j):
+        src, h = j // 2, j % 2
+        v = acc.at[(0, *mine(h))]
+        remote(v, ly.at[src, h], l_y.at[h, 0], l_yr.at[src, h], beside(0)).wait_recv()
+    each(0, 4, got_first)
+    each(0, 4, lambda j: swap(j).wait())
+    for h in (0, 1):
+        r, c = mine(h, qx)
+        gl[0, r, c] = ly[0, h] + ly[1, h]
+        gl[1:3, r, c] = lx[0, h] + lx[1, h]
+    exchange(axis_part(gl, l_ag, 0), 6, lambda: service(1))
+    lead, others = gl.at[pl.ds(0, 1)], gl.at[pl.ds(1, 2)]
+    wide, late_wide = axis_part(lead, l_ag, 1), axis_part(others, l_agb, 1)
+    late_core = core_part(others, l_agbc)
+    each(0, 6, lambda j: wide(j).start())
+    each(0, 6, lambda j: late_wide(j).start())
+    service(2)
+    each(0, 6, lambda j: wide(j).wait())
+    exchange(core_part(lead, l_agc), 1, lambda: service(1))
+
+    sq[1] = ge[1]
+    sq[2] = gl[0] * scale
+
+    def pick(i, a, b, c, d):
+        return jnp.where(i == 0, a, jnp.where(i == 1, b, jnp.where(i == 2, c, d)))
+
+    def products(i, _):
+        @pl.when((i == 0) | (y >= 2))
+        def _():
+            p = mm(sq[pick(i, 0, 0, 5, 6)], sq[pick(i, 2, 3, 10, 11)])
+            p = jnp.where(i == 3, sq[7] - p, p)
+            sq[pick(i, 6, 7, 8, 12)] = p
+            q = mm(sq[pick(i, 6, 6, 5, 0)], p, 0, 0)
+            q = jnp.where(i < 2, sq[pick(i, 1, 4, 4, 4)] - q, q)
+            sq[pick(i, 9, 10, 11, 13)] = q
+
+        @pl.when(i == 0)
+        def _():
+            each(0, 6, lambda j: late_wide(j).wait())
+            late_core(0).start()
+            factor(sq.at[9], u2, sq.at[5], parts, us, ls, hooked(sent[0], passed[0]))
+            late_core(0).wait()
+            sq[3] = gl[1] * scale
+            sq[4] = gl[2] * scale
+        return 0
+
+    lax.fori_loop(0, 4, products, 0)
     sent[0], passed[0] = min(sent[0] + 4, PIECES), min(passed[0] + 4, PIECES)
     source(PIECES)
-    c0j = mm(li1[...], gl[1] * scale)
-    c01 = t1[...]
-    coeff2 = mm(li2[...], gl[2] * scale - mm(c01, c0j, 0, 0))
-    zero = jnp.zeros((PANEL, PANEL), F32)
 
     @pl.when(y == 0)
     def _():
-        upper_ref[:PANEL] = u1[...]
-        upper_ref[PANEL:] = zero
-        m1[...] = li1[...].T
+        m1[...] = sq[0].T
 
     @pl.when(y == 1)
     def _():
-        upper_ref[:PANEL] = t1[...]
-        upper_ref[PANEL:] = u2[...]
-        m1[...] = li2[...].T
-        m2[...] = mm(mm(li1[...], t1[...], 0, 0), li2[...], 1, 1)
+        m1[...] = sq[5].T
+        m2[...] = -mm(mm(sq[0], sq[6], 0, 0), m1[...])
 
     @pl.when(y >= 2)
     def _():
-        upper_ref[:PANEL] = c0j
-        upper_ref[PANEL:] = coeff2
-        zz = mm(li2[...], coeff2, 0, 0)
-        yy = mm(li1[...], c0j - mm(c01, zz), 0, 0)
-
-        @pl.when(y == 2)
-        def _():
-            m1[...] = zz
-            m2[...] = yy
-
-        @pl.when(y == 3)
-        def _():
-            m1[...] = yy
-            m2[...] = zz
+        m1[...] = -sq[jnp.where(y == 2, 11, 13)]
+        m2[...] = -sq[jnp.where(y == 2, 13, 11)]
+
+    @pl.when(y == 0)
+    def _():
+        mcat[: len(TERMS) * PANEL] = stacked([three(m1[...])], 1, 0)
+
+    @pl.when(y >= 1)
+    def _():
+        mcat[...] = stacked([three(m1[...]), three(m2[...])], 1, 0)
 
     per = APPLY // CHUNK
     steps = ROWS // APPLY
@@ -495,7 +506,8 @@
     @pl.when(y == 0)
     def _():
         def go(g):
-            out[part(g), :] = mm(own[part(g), :], m1[...])
+            a = stacked([three(own[part(g), :])], 0, 1)
+            out[part(g), :] = jnp.dot(a, mcat[: len(TERMS) * PANEL], preferred_element_type=F32)
             store(g).start()
         each(0, steps, go)
 
@@ -504,7 +516,8 @@
         def go(i):
             g = (i + steps // 2) % steps
             pl.when(g < steps // 2)(lambda: each(per * g, per * g + per, lambda j: to_side(j, own).wait_recv()))
-            out[part(g), :] = mm(own[part(g), :], m1[...]) - mm(S[part(g), :], m2[...])
+            a = stacked([three(own[part(g), :]), three(S[part(g), :])], 0, 1)
+            out[part(g), :] = jnp.dot(a, mcat[...], preferred_element_type=F32)
             store(g).start()
         each(0, steps, go)
 
@@ -513,13 +526,31 @@
     @pl.when(y >= 2)
     def _():
         def reach(g):
-            return jnp.minimum(jnp.maximum(done + g // 3, per * g + per), PIECES)
+            return jnp.minimum(jnp.maximum(done + g, per * g + per), PIECES)
         def go(g):
             each(jnp.where(g == 0, done, reach(g - 1)), reach(g), forward)
             pl.when(g >= steps // 2)(lambda: each(per * g, per * g + per, lambda j: to_side(j, X).wait_recv()))
-            out[part(g), :] = (own[part(g), :] - mm(X[part(g), :], m1[...])) - mm(S[part(g), :], m2[...])
+            a = stacked([three(X[part(g), :]), three(S[part(g), :])], 0, 1)
+            out[part(g), :] = own[part(g), :] + jnp.dot(a, mcat[...], preferred_element_type=F32)
             store(g).start()
         each(0, steps, go)
+
+    @pl.when(y == 0)
+    def _():
+        upper_ref[:PANEL] = u1[...]
+        upper_ref[PANEL:] = jnp.zeros((PANEL, PANEL), F32)
+
+    @pl.when(y == 1)
+    def _():
+        upper_ref[:PANEL] = sq[6]
+        upper_ref[PANEL:] = u2[...]
+
+    @pl.when(y >= 2)
+    def _():
+        upper_ref[:PANEL] = sq[7]
+        upper_ref[PANEL:] = sq[8]
+
+    pl.when(y % 2 == 1)(lambda: each(0, 8, lambda j: first_send(j).wait_send()))
 
     @pl.when(y < 2)
     def _():
@@ -546,14 +577,15 @@
         scratch_shapes=[
             vmem(ROWS, PANEL), vmem(ROWS, PANEL), vmem(ROWS, PANEL), vmem(ROWS, PANEL),
             vmem(1, PANEL, PANEL), vmem(2, PANEL, PANEL), vmem(3, PANEL, PANEL), vmem(3, PANEL, PANEL),
-            block, block, block, block, block, block, block, block,
+            block, block, block, block, pltpu.VMEM((2 * len(TERMS) * PANEL, PANEL), BF16), vmem(14, PANEL, PANEL),
             vmem(2, HALF, HALF), vmem(2, HALF, HALF), vmem(2, HALF, HALF),
             vmem(1, HALF, PANEL), vmem(2, 3, 1, 32, HALF), vmem(2, 3, 1, 8, HALF),
             vmem(3, HALF, PANEL), vmem(2, 3, 3, 32, HALF), vmem(2, 3, 3, 8, HALF),
-            vmem(2, 2, 8, HALF), vmem(2, 2, 8, HALF),
+            vmem(2, 2, 8, HALF), vmem(2, 2, 2, 8, HALF),
             dma(4), dma(ROWS // APPLY), dma(PIECES), dma(PIECES), dma(PIECES), dma(PIECES),
-            dma(2), dma(2, 2, 2, 3), dma(2, 3), dma(2, 2), dma(2, 2, 2, 3), dma(2),
-            dma(2), dma(2, 2, 2, 3), dma(2, 3), dma(2, 2), dma(2, 2), dma(2, 2, 2, 3), dma(2),
+            dma(2), dma(2, 2, 2, 3), dma(2, 4), dma(2, 2), dma(2, 2, 2, 3), dma(2),
+            dma(2), dma(2, 2, 2, 3), dma(2, 4), dma(2, 2), dma(2, 2, 2), dma(2, 2, 2, 3), dma(2),
+            dma(2, 2, 2, 3), dma(2),
         ],
         compiler_params=pltpu.CompilerParams(
             collective_id=0, has_side_effects=True, vmem_limit_bytes=56 * 2**20

time: 131 us -> 123 us (0.939)
  Pallas kernels: 124 us -> 117 us
    pallas_call x1, Pallas kernels: 124 us -> 117 us  [on_device(): pl.pallas_call(functools.partial(kernel, 1.0 / total_rows), name='factor_...]
where the time goes in v3:
time: 123 us
  Pallas kernels  117 us (95%)
  local copies, waits for them, and re-layouts  5.33 us (4%)
    pallas_call x1, Pallas kernels, on_device(): pl.pallas_call(functools.partial(kernel, 1.0 / total_rows), name='factor_...  117 us
    unnamed x4, local copies, waits for them, and re-layouts  5.33 us

profile of v3, /device:TPU:17, one launch (start us, length us, event | category | flops | bytes accessed | tf_op | source)
XLA Modules:
  0.0 123.1 jit_solution(7271198149243731695)
XLA Ops:
  0.6 117.1 %factor_panels.1 = (f32[4096,256]{1,0:T(8,128)}, f32[512,256]{1,0:T(8,128)}) custom-call(f32[4096,256]{1,0:T(8,128)} %a_hbm.1), custom_call_target="tpu_custom_call" | custom-call | tf_op jit(solution)/shard_map/factor_panels/pallas_call | solution.py:571
  117.7 0.0 copy-start
  117.7 4.5 %copy.5 = f32[4096,256]{1,0:T(8,128)} copy(f32[4096,256]{1,0:T(8,128)} %get-tuple-element.4) | data formatting | bytes 8388608
  122.3 0.0 copy-done
  122.3 0.8 copy.6
Async XLA Ops:
  117.7 4.5 %copy-start = (f32[512,256]{1,0:T(8,128)S(1)}, f32[512,256]{1,0:T(8,128)}, u32[]{:S(2)}) copy-start(f32[512,256]{1,0:T(8,128)} %get-tuple-element.5) | copy-start | bytes 1572868

commit v4 on v3

--- a/solution.py
+++ b/solution.py
@@ -132,10 +132,10 @@
 
 
 def kernel(scale, a_hbm, out_hbm, upper_ref,
-           own, X, S, out, gown, ge, acc, gl, u1, u2, m1, m2, mcat, sq, parts, us, ls,
-           ec, ea, eb, lc, la, lb, ly, lx,
+           own, X, S, out, gown, ge, acc, accs, gl, u1, u2, m1, m2, mcat, sq, parts, us, ls,
+           ec, ea, eb, lc, la, lb, mc, ma, mb, ly, lx,
            load_sem, out_sem, xs, xr, ss, sr,
-           e_core, e_rs, e_y, e_yr, e_ag, e_agc, l_core, l_rs, l_y, l_yr, l_x, l_ag, l_agc, l_agb, l_agbc):
+           e_core, e_rs, e_y, e_yr, e_ag, e_agc, l_core, l_rs, l_y, l_yr, l_x, l_ag, l_agc, l_agb, l_agbc, m_core, m_rs):
     row, y = lax.axis_index("row"), lax.axis_index("col")
     px, pz, k = row // 8, (row // 2) % 4, row % 2
     qx = px + 1 - 2 * (px % 2)
@@ -261,7 +261,7 @@
         pause()
         each(0, n, lambda j: make(j).wait())
 
-    def scatter(ref, bc, ba, bb, sem_core, sem_rs, pauses):
+    def scatter(ref, bc, ba, bb, sem_core, sem_rs):
         def halves(j):
             away = pl.ds(pl.multiple_of(HALF * (1 - k), HALF), HALF)
             return remote(ref.at[:, away], bc, sem_core.at[0], sem_core.at[1], other)
@@ -278,14 +278,25 @@
             return remote(ref.at[:, rows_b(h, to), lanes(h)], bb.at[h, d],
                           sem_rs.at[1, 0, h, d], sem_rs.at[1, 1, h, d], on_axis(1 - h, to))
 
-        exchange(halves, 1, pauses[0])
-        ref[:, pl.ds(base, HALF), :] += bc[...]
-        exchange(wide, 6, pauses[1])
-        for h in (0, 1):
-            ref[:, rows_a(h, first(h)), HALF * h : HALF * h + HALF] += (ba[h, 0] + ba[h, 1]) + ba[h, 2]
-        exchange(narrow, 6, pauses[2])
-        for h in (0, 1):
-            ref[:, rows_b(h, second(h)), HALF * h : HALF * h + HALF] += (bb[h, 0] + bb[h, 1]) + bb[h, 2]
+        def add_half():
+            ref[:, pl.ds(base, HALF), :] += bc[...]
+
+        def add_wide():
+            for h in (0, 1):
+                ref[:, rows_a(h, first(h)), HALF * h : HALF * h + HALF] += (ba[h, 0] + ba[h, 1]) + ba[h, 2]
+
+        def add_narrow():
+            for h in (0, 1):
+                ref[:, rows_b(h, second(h)), HALF * h : HALF * h + HALF] += (bb[h, 0] + bb[h, 1]) + bb[h, 2]
+
+        return (halves, 1, add_half), (wide, 6, add_wide), (narrow, 6, add_narrow)
+
+    def begin(stage):
+        each(0, stage[1], lambda j: stage[0](j).start())
+
+    def finish(stage):
+        each(0, stage[1], lambda j: stage[0](j).wait())
+        stage[2]()
 
     def axis_part(ref, sem_ag, stage):
         def make(j):
@@ -321,15 +332,19 @@
             pl.when(g % 8 == 7)(lambda: new_piece(6 + g // 8))
         each(0, ROWS // GROUP, go)
         sent[0] = 8
-        scatter(gown, ec, ea, eb, e_core, e_rs, [lambda: source(1)] * 3)
+        for stage in scatter(gown, ec, ea, eb, e_core, e_rs):
+            begin(stage)
+            source(1)
+            finish(stage)
 
     acc[...] = jnp.zeros_like(acc)
+    accs[...] = jnp.zeros_like(accs)
 
     def inner(g):
         def two(a, b, c):
             both = mm(jnp.concatenate([group(g, a), group(g, b)], axis=1), group(g, c), 0, 0)
-            acc[1] += both[:PANEL]
-            acc[2] += both[PANEL:]
+            accs[0] += both[:PANEL]
+            accs[1] += both[PANEL:]
 
         def one(a, b):
             acc[0] += mm(group(g, a), group(g, b), 0, 0)
@@ -407,18 +422,31 @@
     sent[0], passed[0] = 22, 17
     sink(EXTRA)
 
-    scatter(acc, lc, la, lb, l_core, l_rs, [lambda: service(1), lambda: service(2), lambda: service(1)])
+    lead = scatter(acc, lc, la, lb, l_core, l_rs)
+    rest = scatter(accs, mc, ma, mb, m_core, m_rs)
+    begin(lead[0])
+    begin(rest[0])
+    for n, pieces in ((0, 1), (1, 2)):
+        service(pieces)
+        finish(lead[n])
+        begin(lead[n + 1])
+        finish(rest[n])
+        begin(rest[n + 1])
+    service(1)
+    finish(lead[2])
+
     def swap(j):
         h, far = j // 2, j % 2
         r, c = mine(h)
         to = ((qx * 4 + pz) * 2 + k, jnp.where(far == 1, 3 - y, y))
-        return remote(acc.at[pl.ds(1, 2), r, c], lx.at[far, h], l_x.at[0, far, h], l_x.at[1, far, h], to)
+        return remote(accs.at[:, r, c], lx.at[far, h], l_x.at[0, far, h], l_x.at[1, far, h], to)
 
     def first_send(j):
         h, d = j // 4, j % 4
         return remote(acc.at[(0, *mine(h))], ly.at[y // 2, h], l_y.at[h, d], l_yr.at[y // 2, h], beside(d))
 
     pl.when(y % 2 == 1)(lambda: each(0, 8, lambda j: first_send(j).start()))
+    finish(rest[2])
     each(0, 4, lambda j: swap(j).start())
     service(2)
 
@@ -427,20 +455,27 @@
         v = acc.at[(0, *mine(h))]
         remote(v, ly.at[src, h], l_y.at[h, 0], l_yr.at[src, h], beside(0)).wait_recv()
     each(0, 4, got_first)
+    for h in (0, 1):
+        r, c = mine(h, qx)
+        gl[0, r, c] = ly[0, h] + ly[1, h]
+    front, others = gl.at[pl.ds(0, 1)], gl.at[pl.ds(1, 2)]
+    near, wide = axis_part(front, l_ag, 0), axis_part(front, l_ag, 1)
+    late_near, late_wide = axis_part(others, l_agb, 0), axis_part(others, l_agb, 1)
+    late_core = core_part(others, l_agbc)
+    each(0, 6, lambda j: near(j).start())
     each(0, 4, lambda j: swap(j).wait())
     for h in (0, 1):
         r, c = mine(h, qx)
-        gl[0, r, c] = ly[0, h] + ly[1, h]
         gl[1:3, r, c] = lx[0, h] + lx[1, h]
-    exchange(axis_part(gl, l_ag, 0), 6, lambda: service(1))
-    lead, others = gl.at[pl.ds(0, 1)], gl.at[pl.ds(1, 2)]
-    wide, late_wide = axis_part(lead, l_ag, 1), axis_part(others, l_agb, 1)
-    late_core = core_part(others, l_agbc)
+    each(0, 6, lambda j: late_near(j).start())
+    service(1)
+    each(0, 6, lambda j: near(j).wait())
     each(0, 6, lambda j: wide(j).start())
+    each(0, 6, lambda j: late_near(j).wait())
     each(0, 6, lambda j: late_wide(j).start())
     service(2)
     each(0, 6, lambda j: wide(j).wait())
-    exchange(core_part(lead, l_agc), 1, lambda: service(1))
+    exchange(core_part(front, l_agc), 1, lambda: service(1))
 
     sq[1] = ge[1]
     sq[2] = gl[0] * scale
@@ -562,6 +597,24 @@
         each(0, PIECES, lambda j: to_side(j, X).wait_send())
 
     each(0, steps, lambda g: store(g).wait())
+
+
+PLACED = 4
+
+
+def place(a_ref, b_ref, out_ref, upper_ref, a_buf, b_buf, sems):
+    step = ROWS // PLACED
+    pairs = [(a_ref.at[pl.ds(i * step, step)], a_buf.at[pl.ds(i * step, step)], out_ref.at[pl.ds(i * step, step)])
+             for i in range(PLACED)] + [(b_ref, b_buf, upper_ref)]
+    ins = [pltpu.make_async_copy(s, b, sems.at[0, i]) for i, (s, b, _) in enumerate(pairs)]
+    outs = [pltpu.make_async_copy(b, d, sems.at[1, i]) for i, (_, b, d) in enumerate(pairs)]
+    for c in ins:
+        c.start()
+    for c, d in zip(ins, outs):
+        c.wait()
+        d.start()
+    for d in outs:
+        d.wait()
 
 
 def on_device(total_rows, influence):
@@ -576,22 +629,32 @@
         out_specs=[pl.BlockSpec(memory_space=pl.ANY)] + [pl.BlockSpec(memory_space=pltpu.VMEM)],
         scratch_shapes=[
             vmem(ROWS, PANEL), vmem(ROWS, PANEL), vmem(ROWS, PANEL), vmem(ROWS, PANEL),
-            vmem(1, PANEL, PANEL), vmem(2, PANEL, PANEL), vmem(3, PANEL, PANEL), vmem(3, PANEL, PANEL),
+            vmem(1, PANEL, PANEL), vmem(2, PANEL, PANEL), vmem(1, PANEL, PANEL), vmem(2, PANEL, PANEL),
+            vmem(3, PANEL, PANEL),
             block, block, block, block, pltpu.VMEM((2 * len(TERMS) * PANEL, PANEL), BF16), vmem(14, PANEL, PANEL),
             vmem(2, HALF, HALF), vmem(2, HALF, HALF), vmem(2, HALF, HALF),
             vmem(1, HALF, PANEL), vmem(2, 3, 1, 32, HALF), vmem(2, 3, 1, 8, HALF),
-            vmem(3, HALF, PANEL), vmem(2, 3, 3, 32, HALF), vmem(2, 3, 3, 8, HALF),
+            vmem(1, HALF, PANEL), vmem(2, 3, 1, 32, HALF), vmem(2, 3, 1, 8, HALF),
+            vmem(2, HALF, PANEL), vmem(2, 3, 2, 32, HALF), vmem(2, 3, 2, 8, HALF),
             vmem(2, 2, 8, HALF), vmem(2, 2, 2, 8, HALF),
             dma(4), dma(ROWS // APPLY), dma(PIECES), dma(PIECES), dma(PIECES), dma(PIECES),
             dma(2), dma(2, 2, 2, 3), dma(2, 4), dma(2, 2), dma(2, 2, 2, 3), dma(2),
             dma(2), dma(2, 2, 2, 3), dma(2, 4), dma(2, 2), dma(2, 2, 2), dma(2, 2, 2, 3), dma(2),
-            dma(2, 2, 2, 3), dma(2),
+            dma(2, 2, 2, 3), dma(2), dma(2), dma(2, 2, 2, 3),
         ],
         compiler_params=pltpu.CompilerParams(
             collective_id=0, has_side_effects=True, vmem_limit_bytes=56 * 2**20
         ),
     )(influence)
-    return factored, upper
+    return pl.pallas_call(
+        place,
+        name="place_results",
+        out_shape=[jax.ShapeDtypeStruct((ROWS, PANEL), F32), jax.ShapeDtypeStruct((2 * PANEL, PANEL), F32)],
+        in_specs=[pl.BlockSpec(memory_space=pl.ANY)] * 2,
+        out_specs=[pl.BlockSpec(memory_space=pl.ANY)] * 2,
+        scratch_shapes=[vmem(ROWS, PANEL), vmem(2 * PANEL, PANEL), dma(2, PLACED + 1)],
+        compiler_params=pltpu.CompilerParams(vmem_limit_bytes=60 * 2**20),
+    )(factored, upper)
 
 
 def solution(mesh):

time: 123 us -> 120 us (0.976)
  local copies, waits for them, and re-layouts: 5.33 us -> 0 us
  Pallas kernels: 117 us -> 119 us
    unnamed x4 -> x0, local copies, waits for them, and re-layouts: 5.33 us -> none
    pallas_call x0 -> x1, Pallas kernels: none -> 3.63 us  [on_device(): pl.pallas_call(place, name='place_results', out_shape=[jax.ShapeDtypeStru...]
    pallas_call x1, Pallas kernels: 117 us -> 115 us  [on_device(): pl.pallas_call(functools.partial(kernel, 1.0 / total_rows), name='factor_...]
where the time goes in v4:
time: 120 us
  Pallas kernels  119 us (99%)
    pallas_call x1, Pallas kernels, on_device(): pl.pallas_call(functools.partial(kernel, 1.0 / total_rows), name='factor_...  115 us
    pallas_call x1, Pallas kernels, on_device(): pl.pallas_call(place, name='place_results', out_shape=[jax.ShapeDtypeStru...  3.63 us

profile of v4, /device:TPU:17, one launch (start us, length us, event | category | flops | bytes accessed | tf_op | source)
XLA Modules:
  0.0 119.8 jit_solution(14436984051561790073)
XLA Ops:
  0.6 115.4 %factor_panels.1 = (f32[4096,256]{1,0:T(8,128)}, f32[512,256]{1,0:T(8,128)}) custom-call(f32[4096,256]{1,0:T(8,128)} %a_hbm.1), custom_call_target="tpu_custom_call" | custom-call | tf_op jit(solution)/shard_map/factor_panels/pallas_call | solution.py:624
  116.0 3.6 %place_results.1 = (f32[4096,256]{1,0:T(8,128)}, f32[512,256]{1,0:T(8,128)}) custom-call(f32[4096,256]{1,0:T(8,128)} %get-tuple-element.4.a_ref, f32[512,256]{1,0:T(8,128)} %get-tuple-element.5.b_ref), custom_call_target="tpu_custom_call" | custom-call | tf_op jit(solution)/shard_map/place_results/pallas_call | solution.py:649

commit v5 on v4

--- a/solution.py
+++ b/solution.py
@@ -16,7 +16,6 @@
 PIECES = ROWS // CHUNK
 EARLY = PIECES // 2
 GROUP = 256
-EXTRA = 1
 LAG = 6
 APPLY = 512
 
@@ -132,7 +131,7 @@
 
 
 def kernel(scale, a_hbm, out_hbm, upper_ref,
-           own, X, S, out, gown, ge, acc, accs, gl, u1, u2, m1, m2, mcat, sq, parts, us, ls,
+           own, X, S, out, gown, ge, acc, accs, gl, u1, u2, m1, mcat, sq, parts, us, ls,
            ec, ea, eb, lc, la, lb, mc, ma, mb, ly, lx,
            load_sem, out_sem, xs, xr, ss, sr,
            e_core, e_rs, e_y, e_yr, e_ag, e_agc, l_core, l_rs, l_y, l_yr, l_x, l_ag, l_agc, l_agb, l_agbc, m_core, m_rs):
@@ -374,7 +373,6 @@
     pl.when(y < 2)(lambda: each(0, 8, lambda j: shard_send(j).start()))
     source(1)
     sink(2)
-    QUARTER = EARLY // 4
 
     def step(i, _):
         @pl.when(y < 2)
@@ -383,16 +381,22 @@
             def got(j):
                 to_across(j).wait_recv()
                 to_side(j, own).wait_recv()
-            each(EARLY + QUARTER * i, EARLY + QUARTER * i + QUARTER, got)
-            each(8 + 2 * i, 10 + 2 * i, inner)
+
+            def tile(t):
+                each(2 * t, 2 * t + 2, got)
+                inner(t)
+            each(8 + 2 * i, 10 + 2 * i, tile)
             pl.when(i < 2)(lambda: new_piece(13 + 2 * i))
 
         @pl.when(y >= 2)
         def _():
             pl.when(i == 0)(lambda: each(2, 4, forward))
             pl.when(i == 1)(lambda: forward(7))
-            each(QUARTER * i, QUARTER * i + QUARTER, lambda j: to_side(j, X).wait_recv())
-            each(2 * i, 2 * i + 2, inner)
+
+            def tile(t):
+                each(2 * t, 2 * t + 2, lambda j: to_side(j, X).wait_recv())
+                inner(t)
+            each(2 * i, 2 * i + 2, tile)
             pl.when(i < 2)(lambda: each(4 * i + 4, 4 * i + 6, forward))
             pl.when(i == 2)(lambda: forward(12))
 
@@ -420,7 +424,6 @@
 
     lax.fori_loop(0, 4, step, 0)
     sent[0], passed[0] = 22, 17
-    sink(EXTRA)
 
     lead = scatter(acc, lc, la, lb, l_core, l_rs)
     rest = scatter(accs, mc, ma, mb, m_core, m_rs)
@@ -484,7 +487,7 @@
         return jnp.where(i == 0, a, jnp.where(i == 1, b, jnp.where(i == 2, c, d)))
 
     def products(i, _):
-        @pl.when((i == 0) | (y >= 2))
+        @pl.when(((i == 0) & (y >= 1)) | (y >= 2))
         def _():
             p = mm(sq[pick(i, 0, 0, 5, 6)], sq[pick(i, 2, 3, 10, 11)])
             p = jnp.where(i == 3, sq[7] - p, p)
@@ -509,25 +512,18 @@
 
     @pl.when(y == 0)
     def _():
-        m1[...] = sq[0].T
+        mcat[: len(TERMS) * PANEL] = stacked([three(sq[0].T)], 1, 0)
 
     @pl.when(y == 1)
     def _():
         m1[...] = sq[5].T
-        m2[...] = -mm(mm(sq[0], sq[6], 0, 0), m1[...])
+        m2 = -mm(mm(sq[0], sq[6], 0, 0), m1[...])
+        mcat[...] = stacked([three(m1[...]), three(m2)], 1, 0)
 
     @pl.when(y >= 2)
     def _():
-        m1[...] = -sq[jnp.where(y == 2, 11, 13)]
-        m2[...] = -sq[jnp.where(y == 2, 13, 11)]
-
-    @pl.when(y == 0)
-    def _():
-        mcat[: len(TERMS) * PANEL] = stacked([three(m1[...])], 1, 0)
-
-    @pl.when(y >= 1)
-    def _():
-        mcat[...] = stacked([three(m1[...]), three(m2[...])], 1, 0)
+        of_x, of_s = sq[jnp.where(y == 2, 11, 13)], sq[jnp.where(y == 2, 13, 11)]
+        mcat[...] = stacked([three(-of_x), three(-of_s)], 1, 0)
 
     per = APPLY // CHUNK
     steps = ROWS // APPLY
@@ -631,7 +627,7 @@
             vmem(ROWS, PANEL), vmem(ROWS, PANEL), vmem(ROWS, PANEL), vmem(ROWS, PANEL),
             vmem(1, PANEL, PANEL), vmem(2, PANEL, PANEL), vmem(1, PANEL, PANEL), vmem(2, PANEL, PANEL),
             vmem(3, PANEL, PANEL),
-            block, block, block, block, pltpu.VMEM((2 * len(TERMS) * PANEL, PANEL), BF16), vmem(14, PANEL, PANEL),
+            block, block, block, pltpu.VMEM((2 * len(TERMS) * PANEL, PANEL), BF16), vmem(14, PANEL, PANEL),
             vmem(2, HALF, HALF), vmem(2, HALF, HALF), vmem(2, HALF, HALF),
             vmem(1, HALF, PANEL), vmem(2, 3, 1, 32, HALF), vmem(2, 3, 1, 8, HALF),
             vmem(1, HALF, PANEL), vmem(2, 3, 1, 32, HALF), vmem(2, 3, 1, 8, HALF),

time: 120 us -> 116 us (0.967)
  Pallas kernels: 119 us -> 115 us
    pallas_call x1, Pallas kernels: 115 us -> 112 us  [on_device(): pl.pallas_call(functools.partial(kernel, 1.0 / total_rows), name='factor_...]
where the time goes in v5:
time: 116 us
  Pallas kernels  115 us (99%)
    pallas_call x1, Pallas kernels, on_device(): pl.pallas_call(functools.partial(kernel, 1.0 / total_rows), name='factor_...  112 us
    pallas_call x1, Pallas kernels, on_device(): pl.pallas_call(place, name='place_results', out_shape=[jax.ShapeDtypeStru...  3.63 us

profile of v5, /device:TPU:17, one launch (start us, length us, event | category | flops | bytes accessed | tf_op | source)
XLA Modules:
  0.0 116.1 jit_solution(4752542438425206959)
XLA Ops:
  0.6 111.7 %factor_panels.1 = (f32[4096,256]{1,0:T(8,128)}, f32[512,256]{1,0:T(8,128)}) custom-call(f32[4096,256]{1,0:T(8,128)} %a_hbm.1), custom_call_target="tpu_custom_call" | custom-call | tf_op jit(solution)/shard_map/factor_panels/pallas_call | solution.py:620
  112.3 3.6 %place_results.1 = (f32[4096,256]{1,0:T(8,128)}, f32[512,256]{1,0:T(8,128)}) custom-call(f32[4096,256]{1,0:T(8,128)} %get-tuple-element.4.a_ref, f32[512,256]{1,0:T(8,128)} %get-tuple-element.5.b_ref), custom_call_target="tpu_custom_call" | custom-call | tf_op jit(solution)/shard_map/place_results/pallas_call | solution.py:645

commit v6 on v5

--- a/solution.py
+++ b/solution.py
@@ -130,11 +130,11 @@
     li_ref[HEAD, TAIL] = jnp.zeros((HALF, HALF), F32)
 
 
-def kernel(scale, a_hbm, out_hbm, upper_ref,
+def kernel(scale, a_hbm, out_hbm, upper_hbm,
            own, X, S, out, gown, ge, acc, accs, gl, u1, u2, m1, mcat, sq, parts, us, ls,
            ec, ea, eb, lc, la, lb, mc, ma, mb, ly, lx,
            load_sem, out_sem, xs, xr, ss, sr,
-           e_core, e_rs, e_y, e_yr, e_ag, e_agc, l_core, l_rs, l_y, l_yr, l_x, l_ag, l_agc, l_agb, l_agbc, m_core, m_rs):
+           e_core, e_rs, e_y, e_yr, e_ag, e_agc, l_core, l_rs, l_y, l_yr, l_x, l_ag, l_agc, l_agb, l_agbc, m_core, m_rs, up_sem):
     row, y = lax.axis_index("row"), lax.axis_index("col")
     px, pz, k = row // 8, (row // 2) % 4, row % 2
     qx = px + 1 - 2 * (px % 2)
@@ -525,6 +525,18 @@
         of_x, of_s = sq[jnp.where(y == 2, 11, 13)], sq[jnp.where(y == 2, 13, 11)]
         mcat[...] = stacked([three(-of_x), three(-of_s)], 1, 0)
 
+    pl.when(y == 0)(lambda: sq.__setitem__(8, jnp.zeros((PANEL, PANEL), F32)))
+
+    def uppers(do):
+        def both(top, bottom):
+            do(pltpu.make_async_copy(top, upper_hbm.at[pl.ds(0, PANEL)], up_sem.at[0]))
+            do(pltpu.make_async_copy(bottom, upper_hbm.at[pl.ds(PANEL, PANEL)], up_sem.at[1]))
+        pl.when(y == 0)(lambda: both(u1, sq.at[8]))
+        pl.when(y == 1)(lambda: both(sq.at[6], u2))
+        pl.when(y >= 2)(lambda: both(sq.at[7], sq.at[8]))
+
+    uppers(lambda c: c.start())
+
     per = APPLY // CHUNK
     steps = ROWS // APPLY
 
@@ -566,21 +578,7 @@
             store(g).start()
         each(0, steps, go)
 
-    @pl.when(y == 0)
-    def _():
-        upper_ref[:PANEL] = u1[...]
-        upper_ref[PANEL:] = jnp.zeros((PANEL, PANEL), F32)
-
-    @pl.when(y == 1)
-    def _():
-        upper_ref[:PANEL] = sq[6]
-        upper_ref[PANEL:] = u2[...]
-
-    @pl.when(y >= 2)
-    def _():
-        upper_ref[:PANEL] = sq[7]
-        upper_ref[PANEL:] = sq[8]
-
+    uppers(lambda c: c.wait())
     pl.when(y % 2 == 1)(lambda: each(0, 8, lambda j: first_send(j).wait_send()))
 
     @pl.when(y < 2)
@@ -622,7 +620,7 @@
         name="factor_panels",
         out_shape=[jax.ShapeDtypeStruct((ROWS, PANEL), F32), jax.ShapeDtypeStruct((2 * PANEL, PANEL), F32)],
         in_specs=[pl.BlockSpec(memory_space=pl.ANY)],
-        out_specs=[pl.BlockSpec(memory_space=pl.ANY)] + [pl.BlockSpec(memory_space=pltpu.VMEM)],
+        out_specs=[pl.BlockSpec(memory_space=pl.ANY)] * 2,
         scratch_shapes=[
             vmem(ROWS, PANEL), vmem(ROWS, PANEL), vmem(ROWS, PANEL), vmem(ROWS, PANEL),
             vmem(1, PANEL, PANEL), vmem(2, PANEL, PANEL), vmem(1, PANEL, PANEL), vmem(2, PANEL, PANEL),
@@ -636,7 +634,7 @@
             dma(4), dma(ROWS // APPLY), dma(PIECES), dma(PIECES), dma(PIECES), dma(PIECES),
             dma(2), dma(2, 2, 2, 3), dma(2, 4), dma(2, 2), dma(2, 2, 2, 3), dma(2),
             dma(2), dma(2, 2, 2, 3), dma(2, 4), dma(2, 2), dma(2, 2, 2), dma(2, 2, 2, 3), dma(2),
-            dma(2, 2, 2, 3), dma(2), dma(2), dma(2, 2, 2, 3),
+            dma(2, 2, 2, 3), dma(2), dma(2), dma(2, 2, 2, 3), dma(2),
         ],
         compiler_params=pltpu.CompilerParams(
             collective_id=0, has_side_effects=True, vmem_limit_bytes=56 * 2**20

time: 116 us -> 115 us (level)
  no operation moved by 1% of the time
where the time goes in v6:
time: 115 us
  Pallas kernels  115 us (100%)
    pallas_call x1, Pallas kernels, on_device(): pl.pallas_call(functools.partial(kernel, 1.0 / total_rows), name='factor_...  111 us
    pallas_call x1, Pallas kernels, on_device(): pl.pallas_call(place, name='place_results', out_shape=[jax.ShapeDtypeStru...  3.63 us

profile of v6, /device:TPU:17, one launch (start us, length us, event | category | flops | bytes accessed | tf_op | source)
XLA Modules:
  0.0 115.4 jit_solution(7820080570354837528)
XLA Ops:
  0.6 110.9 %factor_panels.1 = (f32[4096,256]{1,0:T(8,128)}, f32[512,256]{1,0:T(8,128)}) custom-call(f32[4096,256]{1,0:T(8,128)} %a_hbm.1), custom_call_target="tpu_custom_call" | custom-call | tf_op jit(solution)/shard_map/factor_panels/pallas_call | solution.py:618
  111.6 3.6 %place_results.1 = (f32[4096,256]{1,0:T(8,128)}, f32[512,256]{1,0:T(8,128)}) custom-call(f32[4096,256]{1,0:T(8,128)} %get-tuple-element.4.a_ref, f32[512,256]{1,0:T(8,128)} %get-tuple-element.5.b_ref), custom_call_target="tpu_custom_call" | custom-call | tf_op jit(solution)/shard_map/place_results/pallas_call | solution.py:643
